TPU v7x, 32 devices: a whole 2x2x4 slice. The times are simulated.
32 devices in a mesh: prow: 4 (over y, x), pcol: 8 (over z, core).
Axes of the slice: x: 2, y: 2, z: 4, core: 2. Of those that a mesh axis runs over, the one named last changes fastest.
Arguments:
- coupling: float32 [16, 512, 8, 1024], P(None, 'prow', None, 'pcol')
- diagonal: float32 [16, 512], P(None, 'prow'), as said below
Outputs:
- trailing: float32 [16, 512, 8, 1024], P(None, 'prow', None, 'pcol')
Inputs may be any that keep to these rules, and one draw needn't show every extreme that they name: `diagonal`: every entry is positive.
All inputs are finite; a program needn't handle non-finite values.
Results may differ from a plain program's by a relative error of at most 0.00005.
Values sent between devices are 32-bit elements; how exact they have to be, the bound alone decides.
A program may use at most 128 MiB of HBM per device.

v0:
```python
import jax
import jax.numpy as jnp
from jax import lax
from jax.sharding import PartitionSpec as P


def broadcast(block, axis, source):
    block = jnp.where(lax.axis_index(axis) == source, block, jnp.zeros_like(block))
    return lax.psum(block, axis)


def pivot_factor(column, diagonal, panel_step, row_blocks, row_count, col_count):
    block_size = column.shape[1]
    identity = jnp.eye(block_size, dtype=jnp.float32)
    pivot_block = column[panel_step // row_count] + jnp.diag(diagonal[panel_step // row_count])
    shared = broadcast(pivot_block, "prow", panel_step % row_count)
    lower_factor = jnp.linalg.cholesky(shared)
    inverse = lax.linalg.triangular_solve(lower_factor, identity, left_side=True, lower=True)
    solved = jnp.einsum("anr,mr->anm", column, inverse, precision=lax.Precision.HIGHEST)
    block_index = row_blocks[:, None, None]
    panel_rows = jnp.where(
        block_index == panel_step,
        lower_factor[None],
        jnp.where(block_index > panel_step, solved, jnp.float32(0.0)),
    )
    return broadcast(panel_rows, "pcol", panel_step % col_count)


def transposed(panel_rows, col_blocks, row_count):
    rows_dev = panel_rows.shape[0]
    gathered = lax.all_gather(panel_rows, "prow", axis=0, tiled=True)
    gather_index = col_blocks % row_count * rows_dev + col_blocks // row_count
    return jnp.take(gathered, gather_index, axis=0)


def apply_update(trailing, panel_rows, panel_cols):
    product = jnp.einsum("anr,cmr->ancm", panel_rows, panel_cols, precision=lax.Precision.HIGHEST)
    return trailing - product


def on_device(coupling, diagonal):
    rows_dev = coupling.shape[0]
    cols_dev = coupling.shape[2]
    row_count = lax.axis_size("prow")
    col_count = lax.axis_size("pcol")
    prow_place = lax.axis_index("prow")
    pcol_place = lax.axis_index("pcol")
    row_blocks = jnp.arange(rows_dev, dtype=jnp.int32) * row_count + prow_place
    col_blocks = jnp.arange(cols_dev, dtype=jnp.int32) * col_count + pcol_place
    first_rows = pivot_factor(coupling[:, :, 0, :], diagonal, 0, row_blocks, row_count, col_count)
    first_cols = transposed(first_rows, col_blocks, row_count)
    trailing = apply_update(coupling, first_rows, first_cols)
    second_rows = pivot_factor(
        trailing[:, :, 1 // col_count, :], diagonal, 1, row_blocks, row_count, col_count
    )
    second_cols = transposed(second_rows, col_blocks, row_count)
    trailing = apply_update(trailing, second_rows, second_cols)
    keep_rows = (row_blocks >= 2)[:, None, None, None]
    keep_cols = (col_blocks >= 2)[None, None, :, None]
    return jnp.where(keep_rows & keep_cols, trailing, jnp.float32(0.0))


def solution(mesh):
    return jax.shard_map(
        on_device,
        mesh=mesh,
        in_specs=(P(None, "prow", None, "pcol"), P(None, "prow")),
        out_specs=P(None, "prow", None, "pcol"),
        check_vma=False,
    )
```

profile of v0, /device:TPU:29, one launch (start us, length us, event | category | flops | bytes accessed | tf_op | source)
XLA Modules:
  0.0 431.7 jit_solution(12313435845682830989)
XLA Ops:
  7.2 9.3 %copy.25 = f32[16,128,8,128]{1,3,2,0:T(8,128)} copy(f32[16,128,8,128]{3,2,1,0:T(8,128)} %param.7) | data formatting | bytes 16777216 | tf_op args[0]
  16.6 1.5 fusion.17
  18.1 42.0 %all-reduce.5.cloned.1.call-done = f32[128,128]{0,1:T(8,128)} async-done(((f32[128,128]{0,1:T(8,128)}), f32[128,128]{0,1:T(8,128)}) %all-reduce.5.cloned.1.call-update) | async-done | bytes 65552 | tf_op jit(solution)/shard_map/psum | solution.py:9
  60.1 0.9 copy.20
  61.9 11.7 %cholesky.44 = f32[128,128]{1,0:T(8,128)S(1)} custom-call(f32[128,128]{1,0:T(8,128)S(1)} %fusion.22), custom_call_target="Cholesky" | custom-call | tf_op jit(solution)/shard_map/jit(cholesky)/cholesky | solution.py:17
  75.0 9.8 %custom-call.6 = f32[1,128,128]{1,2,0:T(8,128)S(1)} custom-call(f32[1,128,128]{2,1,0:T(8,128)S(1)} %get-tuple-element.10), custom_call_target="InvertDiagBlocksLowerTriangular" | custom-call | tf_op jit(solution)/shard_map/triangular_solve/custom-call.0 | solution.py:18
  85.2 2.1 fusion.2
  87.3 56.5 %all-reduce.7.cloned.1.call-done = f32[16,128,128]{1,2,0:T(8,128)} async-done(((f32[16,128,128]{1,2,0:T(8,128)}), f32[16,128,128]{1,2,0:T(8,128)}) %all-reduce.7.cloned.1.call-update) | async-done | bytes 1048592 | tf_op jit(solution)/shard_map/psum | solution.py:9
  143.9 2.6 copy.23
  146.7 54.4 %all-gather.3.cloned.1.call-done = f32[64,128,128]{2,1,0:T(8,128)} async-done(((f32[16,128,128]{2,1,0:T(8,128)}), f32[64,128,128]{2,1,0:T(8,128)}) %all-gather.3.cloned.1.call-update) | async-done | bytes 4194320 | tf_op jit(solution)/shard_map/all_gather | solution.py:31
  201.1 2.8 gather_fusion
  203.9 9.7 %convolution_subtract_fusion = f32[16,128,8,128]{1,3,2,0:T(8,128)S(1)} fusion(f32[16,128,8,128]{1,3,2,0:T(8,128)} %copy.25, f32[16,128,128]{1,2,0:T(8,128)} %all-reduce.7.cloned.1.call-done, f32[8,128,128]{2,1,0:T(8,128)S(1)} %gather_fusion, pred[8]{0:T(512)(128)(4,1)S(1)} %compare_and_fusion), kind=kOutput, calls=%fused_computation.3 | convolution fusion | flops 3223453696 | bytes 18350088 | tf_op jit(solution)/shard_map/anr,cmr->ancm/dot_general | solution.py:37
  213.7 3.4 copy-done
  217.8 41.1 %all-reduce.9.cloned.1.call-done = f32[128,128]{0,1:T(8,128)} async-done(((f32[128,128]{0,1:T(8,128)}), f32[128,128]{0,1:T(8,128)}) %all-reduce.9.cloned.1.call-update) | async-done | bytes 65552 | tf_op jit(solution)/shard_map/psum | solution.py:9
  258.9 0.9 copy.27
  260.7 11.7 %cholesky.55 = f32[128,128]{1,0:T(8,128)S(1)} custom-call(f32[128,128]{1,0:T(8,128)S(1)} %fusion.20), custom_call_target="Cholesky" | custom-call | tf_op jit(solution)/shard_map/jit(cholesky)/cholesky | solution.py:17
  273.7 9.8 %custom-call.7 = f32[1,128,128]{1,2,0:T(8,128)S(1)} custom-call(f32[1,128,128]{2,1,0:T(8,128)S(1)} %get-tuple-element.6), custom_call_target="InvertDiagBlocksLowerTriangular" | custom-call | tf_op jit(solution)/shard_map/triangular_solve/custom-call.0 | solution.py:18
  283.9 3.3 fusion.4
  287.5 56.3 %all-reduce.11.cloned.1.call-done = f32[16,128,128]{1,2,0:T(8,128)} async-done(((f32[16,128,128]{1,2,0:T(8,128)}), f32[16,128,128]{1,2,0:T(8,128)}) %all-reduce.11.cloned.1.call-update) | async-done | bytes 1048592 | tf_op jit(solution)/shard_map/psum | solution.py:9
  343.8 2.5 copy.31
  346.5 54.6 %all-gather.5.cloned.1.call-done = f32[64,128,128]{2,1,0:T(8,128)} async-done(((f32[16,128,128]{2,1,0:T(8,128)}), f32[64,128,128]{2,1,0:T(8,128)}) %all-gather.5.cloned.1.call-update) | async-done | bytes 4194320 | tf_op jit(solution)/shard_map/all_gather | solution.py:31
  401.0 2.8 gather_fusion.1
  403.8 11.8 %subtract_select_fusion = f32[16,128,8,128]{1,3,2,0:T(8,128)} fusion(f32[16,128,8,128]{1,3,2,0:T(8,128)} %copy-done, pred[16,8]{1,0:T(8,128)(4,1)S(1)} %broadcast_and_fusion, f32[16,128,128]{1,2,0:T(8,128)} %all-reduce.11.cloned.1.call-done, f32[8,128,128]{2,1,0:T(8,128)S(1)} %gather_fusion.1, pred[8]{0:T(512)(128)(4,1)S(1)} %compare_and_fusion), kind=kOutput, calls=%fused_computation.2 | convolution fusion | flops 3225550848 | bytes 18350216 | tf_op jit(solution)/shard_map/anr,cmr->ancm/dot_general | solution.py:37
  415.6 9.2 %copy.34 = f32[16,128,8,128]{3,2,1,0:T(8,128)} copy(f32[16,128,8,128]{1,3,2,0:T(8,128)} %subtract_select_fusion) | data formatting | bytes 16777216 | tf_op jit(solution)/shard_map/jit(_where)/select_n | solution.py:60
  (37 shorter events, 7.3 us)
Async XLA Ops:
  6.5 53.6 %all-reduce.5.cloned.1.call-start = ((), (), s32[]{:S(2)}) async-start(), calls=%async_computation | async-start | bytes 131072 | tf_op jit(solution)/shard_map/psum | solution.py:9
  7.2 78.0 %slice-start = ((f32[16,128,8,128]{3,2,1,0:T(8,128)}), f32[16,128,1,128]{3,2,1,0:T(1,128)S(1)}, s32[]{:S(2)}) async-start(f32[16,128,8,128]{3,2,1,0:T(8,128)} %param.7), calls=%async_computation.6 | async-start | bytes 2097152 | tf_op jit(solution)/shard_map/slice | solution.py:50
  18.1 125.8 %all-reduce.7.cloned.1.call-start = ((), (), s32[]{:S(2)}) async-start(), calls=%async_computation.1 | async-start | bytes 2097152 | tf_op jit(solution)/shard_map/psum | solution.py:9
  87.3 113.9 %all-gather.3.cloned.1.call-start = ((), (), s32[]{:S(2)}) async-start(), calls=%async_computation.2 | async-start | bytes 5242880 | tf_op jit(solution)/shard_map/all_gather | solution.py:31
  146.4 112.4 %all-reduce.9.cloned.1.call-start = ((), (), s32[]{:S(2)}) async-start(), calls=%async_computation.3 | async-start | bytes 131072 | tf_op jit(solution)/shard_map/psum | solution.py:9
  213.6 3.4 copy-start
  217.7 126.1 %all-reduce.11.cloned.1.call-start = ((), (), s32[]{:S(2)}) async-start(), calls=%async_computation.4 | async-start | bytes 2097152 | tf_op jit(solution)/shard_map/psum | solution.py:9
  287.3 113.8 %all-gather.5.cloned.1.call-start = ((), (), s32[]{:S(2)}) async-start(), calls=%async_computation.5 | async-start | bytes 5242880 | tf_op jit(solution)/shard_map/all_gather | solution.py:31
Sparse Core Ops, SparseCore 0:
  18.2 41.9 all-reduce.4
  87.4 56.4 all-reduce.6
  146.6 54.5 all-gather.2
  217.8 40.9 all-reduce.8
  287.4 56.3 all-reduce.10
  346.5 54.5 all-gather.4
where the time goes:
time: 434 us; the launch traced here: 432 us
  waiting for transfers between devices  305 us (70%)
  other arithmetic  49.7 us (11%)
  local copies, waits for them, and re-layouts  35.3 us (8%)
  matrix products  27.5 us (6%)
  between operations  13.7 us (3%)
    psum x4, waiting for transfers between devices, broadcast(): return lax.psum(block, axis)  196 us
    all_gather x2, waiting for transfers between devices, transposed(): gathered = lax.all_gather(panel_rows, 'prow', axis=0, tiled=True)  109 us
    another operation x6, other arithmetic, pivot_factor(): lower_factor = jnp.linalg.cholesky(shared)  24.8 us
    dot_general x2, matrix products, apply_update(): jnp.einsum('anr,cmr->ancm', panel_rows, panel_cols, precision=lax.Precisi...  21.5 us
    another operation x4, other arithmetic, pivot_factor(): lax.linalg.triangular_solve(lower_factor, identity, left_side=True, lower...  20.9 us
    unnamed x3, local copies, waits for them, and re-layouts  12.7 us
    select_n x1, local copies, waits for them, and re-layouts, on_device(): return jnp.where(keep_rows & keep_cols, trailing, jnp.float32(0.0))  9.24 us
  transfers between devices with their start and end apart: 6, of which 6 were waited for; matrix products, arithmetic and copies ran while one was open for 0% of the time, Pallas kernels for 0%

commit v1 on v0

v1 whole, which is shorter than its diff:
```python
import functools
import math

import jax
import jax.numpy as jnp
from jax import lax
from jax.experimental import pallas as pl
from jax.experimental.pallas import tpu as pltpu
from jax.sharding import PartitionSpec as P

HIGHEST = lax.Precision.HIGHEST
MESH = pl.DeviceIdType.MESH
GROUP = 8
WINDOW = 4
PIECES = 4


def dot(a, b, contract):
    return lax.dot_general(
        a, b, (contract, ((), ())), precision=HIGHEST, preferred_element_type=jnp.float32
    )


def thirds(x):
    first = x.astype(jnp.bfloat16).astype(jnp.float32)
    rest = x - first
    second = rest.astype(jnp.bfloat16).astype(jnp.float32)
    return first, second, rest - second


def eliminate_group(work, group):
    size = work.shape[0]
    start = pl.multiple_of(group * GROUP, GROUP)
    lane = lax.broadcasted_iota(jnp.int32, (GROUP, size), 1) - start
    sub = lax.broadcasted_iota(jnp.int32, (GROUP, size), 0)
    rows = work[pl.ds(start, GROUP), :]
    cols = [
        jnp.broadcast_to(
            jnp.sum(jnp.where(lane == j, rows, 0.0), axis=1, keepdims=True), (GROUP, size)
        )
        for j in range(GROUP)
    ]
    own = (lane >= 0) & (lane < GROUP)
    rows = jnp.where(own, jnp.where(lane == sub, 1.0, 0.0), rows)
    for j in range(GROUP):
        scale = lax.rsqrt(cols[j][j:j + 1, :])
        row = rows[j:j + 1, :] * scale
        column = jnp.where(sub > j, cols[j] * scale, 0.0)
        rows = jnp.where(sub == j, row, rows - column * row)
        for m in range(j + 1, GROUP):
            cols[m] = cols[m] - column * (cols[m][j:j + 1, :] * scale)
    work[pl.ds(start, GROUP), :] = rows
    upper = jnp.where(lane >= GROUP, rows, 0.0)
    a1, a2, a3 = thirds(upper)
    b1, b2, b3 = thirds(rows)
    left = jnp.concatenate([a1, a1, a2, a2, a1, a3], axis=0).astype(jnp.bfloat16)
    right = jnp.concatenate([b1, b2, b1, b2, b3, b1], axis=0).astype(jnp.bfloat16)
    product = lax.dot_general(
        left, right, (((0,), (0,)), ((), ())), preferred_element_type=jnp.float32
    )
    lane_all = lax.broadcasted_iota(jnp.int32, (size, size), 1) - start
    row_all = lax.broadcasted_iota(jnp.int32, (size, size), 0) - start
    dead = (row_all >= GROUP) & (lane_all >= 0) & (lane_all < GROUP)
    work[...] = jnp.where(dead, 0.0, work[...]) - product


def lower_part(x):
    size = x.shape[0]
    row = lax.broadcasted_iota(jnp.int32, (size, size), 0)
    col = lax.broadcasted_iota(jnp.int32, (size, size), 1)
    return jnp.where(row >= col, x, 0.0)


def with_diagonal(block, shift_row):
    size = block.shape[0]
    row = lax.broadcasted_iota(jnp.int32, (size, size), 0)
    col = lax.broadcasted_iota(jnp.int32, (size, size), 1)
    return jnp.where(row == col, block + shift_row, block)


def share_kernel(
    n_prow, n_pcol, width, column, coupling, own_shift, panel, across, pivots, shift,
    local_sem, next_send, next_recv, mate_send, mate_recv,
    pivot_send, pivot_recv, pivot_local, cross_send, cross_recv, shift_send, shift_recv,
):
    p = lax.axis_index("prow")
    q = lax.axis_index("pcol")
    chunks = column.shape[0]
    block = coupling.shape[1]
    height = n_prow // width
    side = q % 2
    mate = q + 1 - 2 * side
    other = 1 - side
    y = p // width
    x = p % width

    barrier = pltpu.get_barrier_semaphore()
    for d in range(1, n_prow):
        pl.semaphore_signal(
            barrier, inc=1, device_id={"prow": (p + d) % n_prow}, device_id_type=MESH
        )
    pl.semaphore_signal(barrier, inc=1, device_id={"pcol": mate}, device_id_type=MESH)

    @pl.when(q >= 2)
    def _():
        pl.semaphore_signal(barrier, inc=1, device_id={"pcol": q - 2}, device_id_type=MESH)

    @pl.when(q + 2 < n_pcol)
    def _():
        pl.semaphore_signal(barrier, inc=1, device_id={"pcol": q + 2}, device_id_type=MESH)

    own_column = pltpu.make_async_copy(column, panel.at[side], local_sem.at[0])
    own_across = pltpu.make_async_copy(coupling.at[0], across.at[p % 2], local_sem.at[1])

    @pl.when(q < 2)
    def _():
        own_column.start()

    @pl.when(p < 2)
    def _():
        own_across.start()

    @pl.when(q < 2)
    def _():
        own_column.wait()

    @pl.when(p < 2)
    def _():
        own_across.wait()

    pl.semaphore_wait(
        barrier,
        n_prow + jnp.where(q >= 2, 1, 0) + jnp.where(q + 2 < n_pcol, 1, 0),
    )

    def to_next(k):
        return pltpu.make_async_remote_copy(
            src_ref=panel.at[side, k], dst_ref=panel.at[side, k],
            send_sem=next_send.at[k], recv_sem=next_recv.at[k],
            device_id={"pcol": jnp.minimum(q + 2, n_pcol - 2 + side)}, device_id_type=MESH,
        )

    def to_mate(k):
        return pltpu.make_async_remote_copy(
            src_ref=panel.at[side, k], dst_ref=panel.at[side, k],
            send_sem=mate_send.at[k], recv_sem=mate_recv.at[k],
            device_id={"pcol": mate}, device_id_type=MESH,
        )

    def from_mate(k):
        return pltpu.make_async_remote_copy(
            src_ref=panel.at[other, k], dst_ref=panel.at[other, k],
            send_sem=mate_send.at[k], recv_sem=mate_recv.at[k],
            device_id={"pcol": mate}, device_id_type=MESH,
        )

    def forward(k):
        @pl.when(q >= 2)
        def _():
            to_next(k).wait_recv()

        @pl.when(q + 2 < n_pcol)
        def _():
            to_next(k).start()

        to_mate(k).start()

    def sent(k):
        @pl.when(q + 2 < n_pcol)
        def _():
            to_next(k).wait_send()

        to_mate(k).wait_send()

    def pivot_copy(i, d, source):
        return pltpu.make_async_remote_copy(
            src_ref=panel.at[source, 0], dst_ref=pivots.at[i],
            send_sem=pivot_send.at[i, d], recv_sem=pivot_recv.at[i],
            device_id={"prow": (p + d) % n_prow}, device_id_type=MESH,
        )

    parts = ((0, 0, 0), (1, 1, 0), (2, 1, 1))

    def shift_copy(i, d):
        return pltpu.make_async_remote_copy(
            src_ref=own_shift, dst_ref=shift.at[i],
            send_sem=shift_send.at[i, d], recv_sem=shift_recv.at[i],
            device_id={"prow": (p + d) % n_prow}, device_id_type=MESH,
        )

    def shift_local(i):
        return pltpu.make_async_copy(own_shift, shift.at[i], local_sem.at[2 + i])

    def cross_copy(s, piece, way):
        rows = block // PIECES
        part = across.at[s, pl.ds(piece * rows, rows)]
        step = (width, 1, -1)[way]
        return pltpu.make_async_remote_copy(
            src_ref=part, dst_ref=part,
            send_sem=cross_send.at[s, piece, way], recv_sem=cross_recv.at[s, piece],
            device_id={"prow": (p + step + n_prow) % n_prow}, device_id_type=MESH,
        )

    def ways(s):
        return (
            (x == s) & (y + 1 < height),
            (x >= s) & (x + 1 < width),
            (x <= s) & (x >= 1),
        )

    def cross(piece):
        for s in (0, 1):
            @pl.when(p != s)
            def _():
                cross_copy(s, piece, 0).wait_recv()

            for way, goes in enumerate(ways(s)):
                @pl.when(goes)
                def _():
                    cross_copy(s, piece, way).start()

    forward(0)
    for i in (0, 1):
        @pl.when(p == i)
        def _():
            for d in range(1, n_prow):
                shift_copy(i, d).start()
            shift_local(i).start()

    from_mate(0).wait_recv()
    for i, owner, source in parts:
        @pl.when(p == owner)
        def _():
            for d in range(1, n_prow):
                pivot_copy(i, d, source).start()
            pltpu.make_async_copy(panel.at[source, 0], pivots.at[i], pivot_local.at[i]).start()

    @pl.loop(1, chunks)
    def _(k):
        forward(k)

        @pl.when(k <= PIECES)
        def _():
            cross(k - 1)

        @pl.when(k >= WINDOW)
        def _():
            sent(k - WINDOW)

    for i, owner, source in parts:
        @pl.when(p == owner)
        def _():
            for d in range(1, n_prow):
                pivot_copy(i, d, source).wait_send()
            pltpu.make_async_copy(panel.at[source, 0], pivots.at[i], pivot_local.at[i]).wait()

        @pl.when(p != owner)
        def _():
            pivot_copy(i, 1, source).wait_recv()

    for i in (0, 1):
        @pl.when(p == i)
        def _():
            for d in range(1, n_prow):
                shift_copy(i, d).wait_send()
            shift_local(i).wait()

        @pl.when(p != i)
        def _():
            shift_copy(i, 1).wait_recv()

    @pl.loop(0, PIECES)
    def _(piece):
        for s in (0, 1):
            for way, goes in enumerate(ways(s)):
                @pl.when(goes)
                def _():
                    cross_copy(s, piece, way).wait_send()

    @pl.loop(chunks - WINDOW, chunks)
    def _(k):
        sent(k)

    @pl.loop(1, chunks)
    def _(k):
        from_mate(k).wait_recv()


def update_kernel(
    n_prow, n_pcol, matrix, panel, across, pivots, shift, out, work, inverse, below, right
):
    step = pl.program_id(0)
    size = panel.shape[-1]
    col_blocks = matrix.shape[1] // size

    @pl.when(step == 0)
    def _():
        def factor(i):
            @pl.loop(0, size // GROUP)
            def _(group):
                eliminate_group(work, group)

            inverse[i] = lower_part(work[...])

        work[...] = with_diagonal(pivots[0], shift[0, 0:1, :])
        factor(0)
        below[...] = dot(pivots[1], inverse[0], ((1,), (1,)))
        work[...] = with_diagonal(pivots[2], shift[1, 0:1, :]) - dot(
            below[...], below[...], ((1,), (1,))
        )
        factor(1)
        for c in range(col_blocks):
            lanes = slice(c * size, (c + 1) * size)
            first = dot(inverse[0], across[0, pl.ds(c, size, stride=col_blocks), :], ((1,), (0,)))
            second = across[1, pl.ds(c, size, stride=col_blocks), :] - dot(
                below[...], first, ((1,), (0,))
            )
            second = dot(inverse[1], second, ((1,), (0,)))
            for i, part in enumerate((first, second)):
                high = part.astype(jnp.bfloat16)
                low = (part - high.astype(jnp.float32)).astype(jnp.bfloat16)
                for j, piece in enumerate((high, low, high)):
                    right[(2 * j + i) * size:(2 * j + i + 1) * size, lanes] = piece

    first = dot(panel[0, 0], inverse[0], ((1,), (1,)))
    second = panel[1, 0] - dot(first, below[...], ((1,), (1,)))
    second = dot(second, inverse[1], ((1,), (1,)))
    left = jnp.concatenate([first, second], axis=1)
    high = left.astype(jnp.bfloat16)
    low = (left - high.astype(jnp.float32)).astype(jnp.bfloat16)
    left = jnp.concatenate([high, high, low], axis=1)
    product = jnp.dot(left, right[...], preferred_element_type=jnp.float32)
    row_kept = step * n_prow + lax.axis_index("prow") >= 2
    q = lax.axis_index("pcol")
    for c in range(col_blocks):
        rows = pl.ds(c, size, stride=col_blocks)
        kept = row_kept & (c * n_pcol + q >= 2)
        value = matrix[0, rows, :] - product[:, c * size:(c + 1) * size]
        out[0, rows, :] = jnp.where(kept, value, 0.0)


def on_device(n_prow, n_pcol, coupling, diagonal):
    chunks, size, col_blocks, _ = coupling.shape
    root = math.isqrt(n_prow)
    width = root if root * root == n_prow else n_prow
    f32 = jnp.float32
    dma = pltpu.SemaphoreType.DMA
    column = coupling[:, :, 0, :]
    own_shift = jnp.broadcast_to(diagonal[0], (8, size))
    panel, across, pivots, shift = pl.pallas_call(
        functools.partial(share_kernel, n_prow, n_pcol, width),
        out_shape=(
            jax.ShapeDtypeStruct((2, chunks, size, size), f32),
            jax.ShapeDtypeStruct((2, size, col_blocks, size), f32),
            jax.ShapeDtypeStruct((3, size, size), f32),
            jax.ShapeDtypeStruct((2, 8, size), f32),
        ),
        in_specs=[pl.BlockSpec(memory_space=pl.ANY)] * 3,
        out_specs=(pl.BlockSpec(memory_space=pl.ANY),) * 4,
        scratch_shapes=[
            dma((4,)), dma((chunks,)), dma((chunks,)), dma((chunks,)), dma((chunks,)),
            dma((3, n_prow)), dma((3,)), dma((3,)),
            dma((2, PIECES, 3)), dma((2, PIECES)), dma((2, n_prow)), dma((2,)),
        ],
        compiler_params=pltpu.CompilerParams(collective_id=0, has_side_effects=True),
        name="share_panels",
    )(column, coupling, own_shift)
    out = pl.pallas_call(
        functools.partial(update_kernel, n_prow, n_pcol),
        grid=(chunks,),
        out_shape=jax.ShapeDtypeStruct((chunks, size * col_blocks, size), f32),
        in_specs=[
            pl.BlockSpec((1, size * col_blocks, size), lambda i: (i, 0, 0)),
            pl.BlockSpec((2, 1, size, size), lambda i: (0, i, 0, 0)),
            pl.BlockSpec((2, size * col_blocks, size), lambda i: (0, 0, 0)),
            pl.BlockSpec((3, size, size), lambda i: (0, 0, 0)),
            pl.BlockSpec((2, 8, size), lambda i: (0, 0, 0)),
        ],
        out_specs=pl.BlockSpec((1, size * col_blocks, size), lambda i: (i, 0, 0)),
        scratch_shapes=[
            pltpu.VMEM((size, size), f32),
            pltpu.VMEM((2, size, size), f32),
            pltpu.VMEM((size, size), f32),
            pltpu.VMEM((6 * size, col_blocks * size), jnp.bfloat16),
        ],
        compiler_params=pltpu.CompilerParams(vmem_limit_bytes=40 * 1024 * 1024),
        name="update_trailing",
    )(
        coupling.reshape(chunks, size * col_blocks, size),
        panel,
        across.reshape(2, size * col_blocks, size),
        pivots,
        shift,
    )
    return out.reshape(coupling.shape)


def solution(mesh):
    return jax.shard_map(
        functools.partial(on_device, mesh.shape["prow"], mesh.shape["pcol"]),
        mesh=mesh,
        in_specs=(P(None, "prow", None, "pcol"), P(None, "prow")),
        out_specs=P(None, "prow", None, "pcol"),
        check_vma=False,
    )
```

time: 434 us -> 167 us (0.38)
  waiting for transfers between devices: 305 us -> 0 us
  Pallas kernels: 0 us -> 153 us
  other arithmetic: 49.7 us -> 0 us
  matrix products: 27.5 us -> 0 us
  local copies, waits for them, and re-layouts: 35.3 us -> 14.1 us
  between operations: 13.7 us -> 0.02 us
    psum x4 -> x0, waiting for transfers between devices: 196 us -> none  [broadcast(): return lax.psum(block, axis)]
    pallas_call x0 -> x2, Pallas kernels: none -> 153 us  [the longest x1 114 us: on_device(): pl.pallas_call(functools.partial(share_kernel, n_prow, n_pcol, width), ou...]
    all_gather x2 -> x0, waiting for transfers between devices: 109 us -> none  [transposed(): gathered = lax.all_gather(panel_rows, 'prow', axis=0, tiled=True)]
    another operation x10 -> x0, other arithmetic: 45.7 us -> none  [the longest x6 24.8 us: pivot_factor(): lower_factor = jnp.linalg.cholesky(shared)]
    dot_general x4 -> x0, matrix products: 26.9 us -> none  [the longest x2 21.5 us: apply_update(): jnp.einsum('anr,cmr->ancm', panel_rows, panel_cols, precision=lax.Precisi...]
    select_n x3 -> x0, local copies, waits for them, and re-layouts: 9.41 us -> none  [the longest x1 9.24 us: on_device(): return jnp.where(keep_rows & keep_cols, trailing, jnp.float32(0.0))]
    psum x4 -> x0, local copies, waits for them, and re-layouts: 6.94 us -> none  [broadcast(): return lax.psum(block, axis)]
    gather x2 -> x0, local copies, waits for them, and re-layouts: 5.53 us -> none  [transposed(): return jnp.take(gathered, gather_index, axis=0)]
  transfers between devices with their start and end apart: 6 -> 0, of which waited for: 6 -> 0; matrix products, arithmetic and copies ran while one was open for 0% -> 0% of each run, Pallas kernels for 0% -> 0%
where the time goes in v1:
time: 167 us
  Pallas kernels  153 us (92%)
  local copies, waits for them, and re-layouts  14.1 us (8%)
    pallas_call x1, Pallas kernels, on_device(): pl.pallas_call(functools.partial(share_kernel, n_prow, n_pcol, width), ou...  114 us
    pallas_call x1, Pallas kernels, on_device(): pl.pallas_call(functools.partial(update_kernel, n_prow, n_pcol), grid=(ch...  38.8 us
    unnamed x10, local copies, waits for them, and re-layouts  7.81 us
    slice x1, local copies, waits for them, and re-layouts, on_device(): column = coupling[:, :, 0, :]  5.02 us

profile of v1, /device:TPU:29, one launch (start us, length us, event | category | flops | bytes accessed | tf_op | source)
XLA Modules:
  0.0 166.7 jit_solution(15228767630790684753)
XLA Ops:
  0.0 0.7 slice_bitcast_fusion
  0.7 0.6 broadcast_in_dim.3.own_shift
  1.3 5.0 %slice.6 = f32[16,128,1,128]{3,2,1,0:T(1,128)} slice(f32[16,128,8,128]{3,2,1,0:T(8,128)} %coupling.1), slice={[0:16], [0:128], [0:1], [0:128]} | slice | bytes 2097152 | tf_op jit(solution)/shard_map/slice | solution.py:348
  6.3 113.8 %share_panels.1 = (f32[2,16,128,128]{3,2,1,0:T(8,128)}, f32[2,128,8,128]{3,2,1,0:T(8,128)}, f32[3,128,128]{2,1,0:T(8,128)}, f32[2,8,128]{2,1,0:T(8,128)}) custom-call(f32[16,128,128]{2,1,0:T(8,128)} %bitcast.10, f32[16,128,8,128]{3,2,1,0:T(8,128)} %coupling.1, f32[8,128]{1,0:T(8,128)} %broadcast_in_dim.3.own_shift), custom_call_target="tpu_custom_call" | custom-call | tf_op jit(solution)/shard_map/share_panels/pallas_call | solution.py:350
  120.1 0.0 copy-start
  120.1 3.4 %copy-done = f32[16,128,8,128]{3,2,1,0:T(8,128)S(1)} copy-done((f32[16,128,8,128]{3,2,1,0:T(8,128)S(1)}, f32[16,128,8,128]{3,2,1,0:T(8,128)}, u32[]{:S(2)}) %copy-start) | copy-done | bytes 8388632
  123.5 0.0 copy-start.1
  123.5 1.6 copy-done.1
  125.0 0.0 copy-start.2
  125.0 1.2 copy-done.2
  126.3 0.0 copy-start.3
  126.3 0.9 copy-done.3
  127.2 0.0 copy-start.4
  127.2 0.7 copy-done.4
  127.9 38.8 %update_trailing.1 = f32[16,1024,128]{2,1,0:T(8,128)} custom-call(f32[16,1024,128]{2,1,0:T(8,128)S(1)} %bitcast.8, f32[2,16,128,128]{3,2,1,0:T(8,128)S(1)} %copy-done.1, f32[2,1024,128]{2,1,0:T(8,128)S(1)} %bitcast.9, f32[3,128,128]{2,1,0:T(8,128)S(1)} %copy-done.3, f32[2,8,128]{2,1,0:T(8,128)S(1)} %copy-done.4), custom_call_target="tpu_custom_call" | custom-call | tf_op jit(solution)/shard_map/update_trailing/pallas_call | solution.py:368
Async XLA Ops:
  120.1 3.4 %copy-start = (f32[16,128,8,128]{3,2,1,0:T(8,128)S(1)}, f32[16,128,8,128]{3,2,1,0:T(8,128)}, u32[]{:S(2)}) copy-start(f32[16,128,8,128]{3,2,1,0:T(8,128)} %coupling.1) | copy-start | bytes 25165828
  123.5 1.6 copy-start.1
  125.0 1.2 copy-start.2
  126.3 0.9 copy-start.3
  127.2 0.7 copy-start.4

commit v2 on v1

--- a/solution.py
+++ b/solution.py
@@ -11,7 +11,6 @@
 HIGHEST = lax.Precision.HIGHEST
 MESH = pl.DeviceIdType.MESH
 GROUP = 8
-WINDOW = 4
 PIECES = 4
 
 
@@ -79,14 +78,13 @@
 
 
 def share_kernel(
-    n_prow, n_pcol, width, column, coupling, own_shift, panel, across, pivots, shift,
-    local_sem, next_send, next_recv, mate_send, mate_recv,
+    n_prow, n_pcol, width, coupling, own_shift, panel, across, inverse, below,
+    pivots, shift, work, local_sem, next_send, next_recv, mate_send, mate_recv,
     pivot_send, pivot_recv, pivot_local, cross_send, cross_recv, shift_send, shift_recv,
 ):
     p = lax.axis_index("prow")
     q = lax.axis_index("pcol")
-    chunks = column.shape[0]
-    block = coupling.shape[1]
+    chunks, block = coupling.shape[:2]
     height = n_prow // width
     side = q % 2
     mate = q + 1 - 2 * side
@@ -109,7 +107,9 @@
     def _():
         pl.semaphore_signal(barrier, inc=1, device_id={"pcol": q + 2}, device_id_type=MESH)
 
-    own_column = pltpu.make_async_copy(column, panel.at[side], local_sem.at[0])
+    own_column = pltpu.make_async_copy(
+        coupling.at[:, :, 0, :], panel.at[side], local_sem.at[0]
+    )
     own_across = pltpu.make_async_copy(coupling.at[0], across.at[p % 2], local_sem.at[1])
 
     @pl.when(q < 2)
@@ -235,39 +235,78 @@
                 pivot_copy(i, d, source).start()
             pltpu.make_async_copy(panel.at[source, 0], pivots.at[i], pivot_local.at[i]).start()
 
-    @pl.loop(1, chunks)
-    def _(k):
-        forward(k)
-
-        @pl.when(k <= PIECES)
-        def _():
-            cross(k - 1)
-
-        @pl.when(k >= WINDOW)
-        def _():
-            sent(k - WINDOW)
+    forward(1)
+    forward(2)
+
+    def arrived(i, owner, source):
+        @pl.when(p == owner)
+        def _():
+            pltpu.make_async_copy(panel.at[source, 0], pivots.at[i], pivot_local.at[i]).wait()
+
+        @pl.when(p != owner)
+        def _():
+            pivot_copy(i, 1, source).wait_recv()
+
+    def shift_arrived(i):
+        @pl.when(p == i)
+        def _():
+            shift_local(i).wait()
+
+        @pl.when(p != i)
+        def _():
+            shift_copy(i, 1).wait_recv()
+
+    def pass_on(slot):
+        k = slot + 3
+
+        @pl.when(k < chunks)
+        def _():
+            forward(k)
+            sent(k - 3)
+
+        @pl.when(slot < PIECES)
+        def _():
+            cross(slot)
+
+    slots = block // (2 * GROUP)
+
+    def factor(i):
+        @pl.loop(0, slots)
+        def _(slot):
+            pass_on(i * slots + slot)
+            eliminate_group(work, 2 * slot)
+            eliminate_group(work, 2 * slot + 1)
+
+        inverse[i] = lower_part(work[...])
+
+    shift_arrived(0)
+    arrived(*parts[0])
+    work[...] = with_diagonal(pivots[0], shift[0, 0:1, :])
+    factor(0)
+    shift_arrived(1)
+    arrived(*parts[1])
+    arrived(*parts[2])
+    below[...] = dot(pivots[1], inverse[0], ((1,), (1,)))
+    work[...] = with_diagonal(pivots[2], shift[1, 0:1, :]) - dot(
+        below[...], below[...], ((1,), (1,))
+    )
+    factor(1)
+
+    @pl.loop(2 * slots, max(chunks - 3, 2 * slots))
+    def _(slot):
+        pass_on(slot)
 
     for i, owner, source in parts:
         @pl.when(p == owner)
         def _():
             for d in range(1, n_prow):
                 pivot_copy(i, d, source).wait_send()
-            pltpu.make_async_copy(panel.at[source, 0], pivots.at[i], pivot_local.at[i]).wait()
-
-        @pl.when(p != owner)
-        def _():
-            pivot_copy(i, 1, source).wait_recv()
 
     for i in (0, 1):
         @pl.when(p == i)
         def _():
             for d in range(1, n_prow):
                 shift_copy(i, d).wait_send()
-            shift_local(i).wait()
-
-        @pl.when(p != i)
-        def _():
-            shift_copy(i, 1).wait_recv()
 
     @pl.loop(0, PIECES)
     def _(piece):
@@ -277,7 +316,7 @@
                 def _():
                     cross_copy(s, piece, way).wait_send()
 
-    @pl.loop(chunks - WINDOW, chunks)
+    @pl.loop(chunks - 3, chunks)
     def _(k):
         sent(k)
 
@@ -287,7 +326,7 @@
 
 
 def update_kernel(
-    n_prow, n_pcol, matrix, panel, across, pivots, shift, out, work, inverse, below, right
+    n_prow, n_pcol, matrix, panel, across, inverse, below, out, right
 ):
     step = pl.program_id(0)
     size = panel.shape[-1]
@@ -295,20 +334,6 @@
 
     @pl.when(step == 0)
     def _():
-        def factor(i):
-            @pl.loop(0, size // GROUP)
-            def _(group):
-                eliminate_group(work, group)
-
-            inverse[i] = lower_part(work[...])
-
-        work[...] = with_diagonal(pivots[0], shift[0, 0:1, :])
-        factor(0)
-        below[...] = dot(pivots[1], inverse[0], ((1,), (1,)))
-        work[...] = with_diagonal(pivots[2], shift[1, 0:1, :]) - dot(
-            below[...], below[...], ((1,), (1,))
-        )
-        factor(1)
         for c in range(col_blocks):
             lanes = slice(c * size, (c + 1) * size)
             first = dot(inverse[0], across[0, pl.ds(c, size, stride=col_blocks), :], ((1,), (0,)))
@@ -345,26 +370,31 @@
     width = root if root * root == n_prow else n_prow
     f32 = jnp.float32
     dma = pltpu.SemaphoreType.DMA
-    column = coupling[:, :, 0, :]
+    vmem = pl.BlockSpec(memory_space=pltpu.VMEM)
     own_shift = jnp.broadcast_to(diagonal[0], (8, size))
-    panel, across, pivots, shift = pl.pallas_call(
+    panel, across, inverse, below = pl.pallas_call(
         functools.partial(share_kernel, n_prow, n_pcol, width),
         out_shape=(
             jax.ShapeDtypeStruct((2, chunks, size, size), f32),
             jax.ShapeDtypeStruct((2, size, col_blocks, size), f32),
-            jax.ShapeDtypeStruct((3, size, size), f32),
-            jax.ShapeDtypeStruct((2, 8, size), f32),
+            jax.ShapeDtypeStruct((2, size, size), f32),
+            jax.ShapeDtypeStruct((size, size), f32),
         ),
-        in_specs=[pl.BlockSpec(memory_space=pl.ANY)] * 3,
-        out_specs=(pl.BlockSpec(memory_space=pl.ANY),) * 4,
+        in_specs=[pl.BlockSpec(memory_space=pl.ANY), vmem],
+        out_specs=(vmem,) * 4,
         scratch_shapes=[
+            pltpu.VMEM((3, size, size), f32),
+            pltpu.VMEM((2, 8, size), f32),
+            pltpu.VMEM((size, size), f32),
             dma((4,)), dma((chunks,)), dma((chunks,)), dma((chunks,)), dma((chunks,)),
             dma((3, n_prow)), dma((3,)), dma((3,)),
             dma((2, PIECES, 3)), dma((2, PIECES)), dma((2, n_prow)), dma((2,)),
         ],
-        compiler_params=pltpu.CompilerParams(collective_id=0, has_side_effects=True),
+        compiler_params=pltpu.CompilerParams(
+            collective_id=0, has_side_effects=True, vmem_limit_bytes=60 * 1024 * 1024
+        ),
         name="share_panels",
-    )(column, coupling, own_shift)
+    )(coupling, own_shift)
     out = pl.pallas_call(
         functools.partial(update_kernel, n_prow, n_pcol),
         grid=(chunks,),
@@ -373,24 +403,21 @@
             pl.BlockSpec((1, size * col_blocks, size), lambda i: (i, 0, 0)),
             pl.BlockSpec((2, 1, size, size), lambda i: (0, i, 0, 0)),
             pl.BlockSpec((2, size * col_blocks, size), lambda i: (0, 0, 0)),
-            pl.BlockSpec((3, size, size), lambda i: (0, 0, 0)),
-            pl.BlockSpec((2, 8, size), lambda i: (0, 0, 0)),
+            pl.BlockSpec((2, size, size), lambda i: (0, 0, 0)),
+            pl.BlockSpec((size, size), lambda i: (0, 0)),
         ],
         out_specs=pl.BlockSpec((1, size * col_blocks, size), lambda i: (i, 0, 0)),
         scratch_shapes=[
-            pltpu.VMEM((size, size), f32),
-            pltpu.VMEM((2, size, size), f32),
-            pltpu.VMEM((size, size), f32),
             pltpu.VMEM((6 * size, col_blocks * size), jnp.bfloat16),
         ],
-        compiler_params=pltpu.CompilerParams(vmem_limit_bytes=40 * 1024 * 1024),
+        compiler_params=pltpu.CompilerParams(vmem_limit_bytes=60 * 1024 * 1024),
         name="update_trailing",
     )(
         coupling.reshape(chunks, size * col_blocks, size),
         panel,
         across.reshape(2, size * col_blocks, size),
-        pivots,
-        shift,
+        inverse,
+        below,
     )
     return out.reshape(coupling.shape)
 

time: 167 us -> 99.1 us (0.59)
  Pallas kernels: 153 us -> 95.9 us
  local copies, waits for them, and re-layouts: 14.1 us -> 1.28 us
    pallas_call x1, Pallas kernels: 114 us -> 67.4 us  [on_device(): pl.pallas_call(functools.partial(share_kernel, n_prow, n_pcol, width), ou...]
    pallas_call x1, Pallas kernels: 38.8 us -> 28.5 us  [on_device(): pl.pallas_call(functools.partial(update_kernel, n_prow, n_pcol), grid=(ch...]
    unnamed x10 -> x0, local copies, waits for them, and re-layouts: 7.81 us -> none
    slice x1 -> x0, local copies, waits for them, and re-layouts: 5.02 us -> none  [on_device(): column = coupling[:, :, 0, :]]
where the time goes in v2:
time: 99.1 us; the launch traced here: 97.2 us
  Pallas kernels  95.9 us (97%)
  local copies, waits for them, and re-layouts  1.28 us (1%)
    pallas_call x1, Pallas kernels, on_device(): pl.pallas_call(functools.partial(share_kernel, n_prow, n_pcol, width), ou...  67.4 us
    pallas_call x1, Pallas kernels, on_device(): pl.pallas_call(functools.partial(update_kernel, n_prow, n_pcol), grid=(ch...  28.5 us

profile of v2, /device:TPU:29, one launch (start us, length us, event | category | flops | bytes accessed | tf_op | source)
XLA Modules:
  0.0 97.2 jit_solution(6956986811133279146)
XLA Ops:
  0.0 0.7 slice_bitcast_fusion
  0.7 0.6 broadcast_in_dim.3.own_shift
  1.3 67.4 %share_panels.1 = (f32[2,16,128,128]{3,2,1,0:T(8,128)}, f32[2,128,8,128]{3,2,1,0:T(8,128)}, f32[2,128,128]{2,1,0:T(8,128)}, f32[128,128]{1,0:T(8,128)}) custom-call(f32[16,128,8,128]{3,2,1,0:T(8,128)} %coupling.1, f32[8,128]{1,0:T(8,128)} %broadcast_in_dim.3.own_shift), custom_call_target="tpu_custom_call" | custom-call | tf_op jit(solution)/shard_map/share_panels/pallas_call | solution.py:375
  68.7 28.5 %update_trailing.1 = f32[16,1024,128]{2,1,0:T(8,128)} custom-call(f32[16,1024,128]{2,1,0:T(8,128)} %bitcast.5, f32[2,16,128,128]{3,2,1,0:T(8,128)} %get-tuple-element.9.panel, f32[2,1024,128]{2,1,0:T(8,128)} %bitcast.6, f32[2,128,128]{2,1,0:T(8,128)} %get-tuple-element.11.inverse, f32[128,128]{1,0:T(8,128)} %get-tuple-element.12.below), custom_call_target="tpu_custom_call" | custom-call | tf_op jit(solution)/shard_map/update_trailing/pallas_call | solution.py:398

commit v3 on v2

--- a/solution.py
+++ b/solution.py
@@ -78,8 +78,8 @@
 
 
 def share_kernel(
-    n_prow, n_pcol, width, coupling, own_shift, panel, across, inverse, below,
-    pivots, shift, work, local_sem, next_send, next_recv, mate_send, mate_recv,
+    n_prow, n_pcol, width, coupling, own_shift, panel, across, inverse,
+    pivots, shift, work, below, stage, stage_sem, local_sem, next_send, next_recv, mate_send, mate_recv,
     pivot_send, pivot_recv, pivot_local, cross_send, cross_recv, shift_send, shift_recv,
 ):
     p = lax.axis_index("prow")
@@ -107,22 +107,20 @@
     def _():
         pl.semaphore_signal(barrier, inc=1, device_id={"pcol": q + 2}, device_id_type=MESH)
 
-    own_column = pltpu.make_async_copy(
-        coupling.at[:, :, 0, :], panel.at[side], local_sem.at[0]
-    )
+    def staged(k):
+        return pltpu.make_async_copy(coupling.at[k], stage.at[k], stage_sem.at[k])
+
     own_across = pltpu.make_async_copy(coupling.at[0], across.at[p % 2], local_sem.at[1])
 
     @pl.when(q < 2)
     def _():
-        own_column.start()
+        @pl.loop(0, chunks)
+        def _(k):
+            staged(k).start()
 
     @pl.when(p < 2)
     def _():
         own_across.start()
-
-    @pl.when(q < 2)
-    def _():
-        own_column.wait()
 
     @pl.when(p < 2)
     def _():
@@ -155,6 +153,11 @@
         )
 
     def forward(k):
+        @pl.when(q < 2)
+        def _():
+            staged(k).wait()
+            panel[side, k] = stage[k, :, 0, :]
+
         @pl.when(q >= 2)
         def _():
             to_next(k).wait_recv()
@@ -277,20 +280,26 @@
             eliminate_group(work, 2 * slot)
             eliminate_group(work, 2 * slot + 1)
 
-        inverse[i] = lower_part(work[...])
+        rows = slice(i * block, (i + 1) * block)
+        inverse[rows, rows] = lower_part(work[...])
+        return inverse[rows, rows]
 
     shift_arrived(0)
     arrived(*parts[0])
     work[...] = with_diagonal(pivots[0], shift[0, 0:1, :])
-    factor(0)
+    first = factor(0)
+    inverse[0:block, block:] = jnp.zeros_like(first)
     shift_arrived(1)
     arrived(*parts[1])
     arrived(*parts[2])
-    below[...] = dot(pivots[1], inverse[0], ((1,), (1,)))
+    below[...] = dot(pivots[1], first, ((1,), (1,)))
     work[...] = with_diagonal(pivots[2], shift[1, 0:1, :]) - dot(
         below[...], below[...], ((1,), (1,))
     )
-    factor(1)
+    second = factor(1)
+    inverse[block:, 0:block] = -dot(
+        second, dot(below[...], inverse[0:block, 0:block], ((1,), (0,))), ((1,), (0,))
+    )
 
     @pl.loop(2 * slots, max(chunks - 3, 2 * slots))
     def _(slot):
@@ -325,43 +334,42 @@
         from_mate(k).wait_recv()
 
 
-def update_kernel(
-    n_prow, n_pcol, matrix, panel, across, inverse, below, out, right
-):
+def halves(x):
+    high = x.astype(jnp.bfloat16)
+    return high, (x - high.astype(jnp.float32)).astype(jnp.bfloat16)
+
+
+def update_kernel(n_prow, n_pcol, matrix, panel, across, inverse, out, right):
     step = pl.program_id(0)
-    size = panel.shape[-1]
-    col_blocks = matrix.shape[1] // size
+    blocks, size, col_blocks, _ = matrix.shape
 
     @pl.when(step == 0)
     def _():
-        for c in range(col_blocks):
-            lanes = slice(c * size, (c + 1) * size)
-            first = dot(inverse[0], across[0, pl.ds(c, size, stride=col_blocks), :], ((1,), (0,)))
-            second = across[1, pl.ds(c, size, stride=col_blocks), :] - dot(
-                below[...], first, ((1,), (0,))
+        panels = [
+            jnp.concatenate(
+                [across[s, pl.ds(c, size, stride=col_blocks), :] for c in range(col_blocks)],
+                axis=1,
             )
-            second = dot(inverse[1], second, ((1,), (0,)))
-            for i, part in enumerate((first, second)):
-                high = part.astype(jnp.bfloat16)
-                low = (part - high.astype(jnp.float32)).astype(jnp.bfloat16)
-                for j, piece in enumerate((high, low, high)):
-                    right[(2 * j + i) * size:(2 * j + i + 1) * size, lanes] = piece
-
-    first = dot(panel[0, 0], inverse[0], ((1,), (1,)))
-    second = panel[1, 0] - dot(first, below[...], ((1,), (1,)))
-    second = dot(second, inverse[1], ((1,), (1,)))
-    left = jnp.concatenate([first, second], axis=1)
-    high = left.astype(jnp.bfloat16)
-    low = (left - high.astype(jnp.float32)).astype(jnp.bfloat16)
+            for s in (0, 1)
+        ]
+        solved = dot(inverse[...], jnp.concatenate(panels, axis=0), ((1,), (0,)))
+        high, low = halves(solved)
+        for j, piece in enumerate((high, low, high)):
+            right[2 * j * size:2 * (j + 1) * size, :] = piece
+
+    raw = jnp.concatenate(
+        [panel[s].reshape(blocks * size, size) for s in (0, 1)], axis=1
+    )
+    high, low = halves(dot(raw, inverse[...], ((1,), (1,))))
     left = jnp.concatenate([high, high, low], axis=1)
     product = jnp.dot(left, right[...], preferred_element_type=jnp.float32)
-    row_kept = step * n_prow + lax.axis_index("prow") >= 2
-    q = lax.axis_index("pcol")
-    for c in range(col_blocks):
-        rows = pl.ds(c, size, stride=col_blocks)
-        kept = row_kept & (c * n_pcol + q >= 2)
-        value = matrix[0, rows, :] - product[:, c * size:(c + 1) * size]
-        out[0, rows, :] = jnp.where(kept, value, 0.0)
+    product = product.reshape(blocks, size, col_blocks, size)
+    p = lax.axis_index("prow")
+    col = lax.broadcasted_iota(jnp.int32, (1, col_blocks, size), 1) * n_pcol
+    cols_kept = col + lax.axis_index("pcol") >= 2
+    for b in range(blocks):
+        kept = cols_kept & ((step * blocks + b) * n_prow + p >= 2)
+        out[b] = jnp.where(kept, matrix[b] - product[b], 0.0)
 
 
 def on_device(n_prow, n_pcol, coupling, diagonal):
@@ -372,21 +380,22 @@
     dma = pltpu.SemaphoreType.DMA
     vmem = pl.BlockSpec(memory_space=pltpu.VMEM)
     own_shift = jnp.broadcast_to(diagonal[0], (8, size))
-    panel, across, inverse, below = pl.pallas_call(
+    panel, across, inverse = pl.pallas_call(
         functools.partial(share_kernel, n_prow, n_pcol, width),
         out_shape=(
             jax.ShapeDtypeStruct((2, chunks, size, size), f32),
             jax.ShapeDtypeStruct((2, size, col_blocks, size), f32),
-            jax.ShapeDtypeStruct((2, size, size), f32),
-            jax.ShapeDtypeStruct((size, size), f32),
+            jax.ShapeDtypeStruct((2 * size, 2 * size), f32),
         ),
         in_specs=[pl.BlockSpec(memory_space=pl.ANY), vmem],
-        out_specs=(vmem,) * 4,
+        out_specs=(vmem,) * 3,
         scratch_shapes=[
             pltpu.VMEM((3, size, size), f32),
             pltpu.VMEM((2, 8, size), f32),
             pltpu.VMEM((size, size), f32),
-            dma((4,)), dma((chunks,)), dma((chunks,)), dma((chunks,)), dma((chunks,)),
+            pltpu.VMEM((size, size), f32),
+            pltpu.VMEM(coupling.shape, f32),
+            dma((chunks,)), dma((4,)), dma((chunks,)), dma((chunks,)), dma((chunks,)), dma((chunks,)),
             dma((3, n_prow)), dma((3,)), dma((3,)),
             dma((2, PIECES, 3)), dma((2, PIECES)), dma((2, n_prow)), dma((2,)),
         ],
@@ -395,31 +404,22 @@
         ),
         name="share_panels",
     )(coupling, own_shift)
-    out = pl.pallas_call(
+    blocks = math.gcd(chunks, 4)
+    return pl.pallas_call(
         functools.partial(update_kernel, n_prow, n_pcol),
-        grid=(chunks,),
-        out_shape=jax.ShapeDtypeStruct((chunks, size * col_blocks, size), f32),
+        grid=(chunks // blocks,),
+        out_shape=jax.ShapeDtypeStruct(coupling.shape, f32),
         in_specs=[
-            pl.BlockSpec((1, size * col_blocks, size), lambda i: (i, 0, 0)),
-            pl.BlockSpec((2, 1, size, size), lambda i: (0, i, 0, 0)),
+            pl.BlockSpec((blocks, size, col_blocks, size), lambda i: (i, 0, 0, 0)),
+            pl.BlockSpec((2, blocks, size, size), lambda i: (0, i, 0, 0)),
             pl.BlockSpec((2, size * col_blocks, size), lambda i: (0, 0, 0)),
-            pl.BlockSpec((2, size, size), lambda i: (0, 0, 0)),
-            pl.BlockSpec((size, size), lambda i: (0, 0)),
+            pl.BlockSpec((2 * size, 2 * size), lambda i: (0, 0)),
         ],
-        out_specs=pl.BlockSpec((1, size * col_blocks, size), lambda i: (i, 0, 0)),
-        scratch_shapes=[
-            pltpu.VMEM((6 * size, col_blocks * size), jnp.bfloat16),
-        ],
+        out_specs=pl.BlockSpec((blocks, size, col_blocks, size), lambda i: (i, 0, 0, 0)),
+        scratch_shapes=[pltpu.VMEM((6 * size, col_blocks * size), jnp.bfloat16)],
         compiler_params=pltpu.CompilerParams(vmem_limit_bytes=60 * 1024 * 1024),
         name="update_trailing",
-    )(
-        coupling.reshape(chunks, size * col_blocks, size),
-        panel,
-        across.reshape(2, size * col_blocks, size),
-        inverse,
-        below,
-    )
-    return out.reshape(coupling.shape)
+    )(coupling, panel, across.reshape(2, size * col_blocks, size), inverse)
 
 
 def solution(mesh):

time: 99.1 us -> 86.3 us (0.87)
  the two profiles are of different devices: /device:TPU:29 before, /device:TPU:28 now
where the time goes in v3:
time: 86.3 us; the launch traced here: 86.1 us
  Pallas kernels  84.8 us (98%)
  local copies, waits for them, and re-layouts  1.28 us (1%)
    pallas_call x1, Pallas kernels, on_device(): pl.pallas_call(functools.partial(share_kernel, n_prow, n_pcol, width), ou...  70.1 us
    pallas_call x1, Pallas kernels, on_device(): pl.pallas_call(functools.partial(update_kernel, n_prow, n_pcol), grid=(ch...  14.7 us

profile of v3, /device:TPU:28, one launch (start us, length us, event | category | flops | bytes accessed | tf_op | source)
XLA Modules:
  0.0 86.1 jit_solution(15545185190074456343)
XLA Ops:
  0.0 0.7 slice_bitcast_fusion
  0.7 0.6 broadcast_in_dim.3.own_shift
  1.3 70.1 %share_panels.1 = (f32[2,16,128,128]{3,2,1,0:T(8,128)}, f32[2,128,8,128]{3,2,1,0:T(8,128)}, f32[256,256]{1,0:T(8,128)}) custom-call(f32[16,128,8,128]{3,2,1,0:T(8,128)} %matrix.1, f32[8,128]{1,0:T(8,128)} %broadcast_in_dim.3.own_shift), custom_call_target="tpu_custom_call" | custom-call | tf_op jit(solution)/shard_map/share_panels/pallas_call | solution.py:383
  71.4 14.7 %update_trailing.1 = f32[16,128,8,128]{3,2,1,0:T(8,128)} custom-call(f32[16,128,8,128]{3,2,1,0:T(8,128)} %matrix.1, f32[2,16,128,128]{3,2,1,0:T(8,128)} %get-tuple-element.8.panel, f32[2,1024,128]{2,1,0:T(8,128)} %bitcast.3, f32[256,256]{1,0:T(8,128)} %get-tuple-element.10.inverse), custom_call_target="tpu_custom_call" | custom-call | tf_op jit(solution)/shard_map/update_trailing/pallas_call | solution.py:408

commit v4 on v3

--- a/solution.py
+++ b/solution.py
@@ -12,6 +12,7 @@
 MESH = pl.DeviceIdType.MESH
 GROUP = 8
 PIECES = 4
+SLOT = 4
 
 
 def dot(a, b, contract):
@@ -25,6 +26,11 @@
     rest = x - first
     second = rest.astype(jnp.bfloat16).astype(jnp.float32)
     return first, second, rest - second
+
+
+def halves(x):
+    high = x.astype(jnp.bfloat16)
+    return high, (x - high.astype(jnp.float32)).astype(jnp.bfloat16)
 
 
 def eliminate_group(work, group):
@@ -78,8 +84,8 @@
 
 
 def share_kernel(
-    n_prow, n_pcol, width, coupling, own_shift, panel, across, inverse,
-    pivots, shift, work, below, stage, stage_sem, local_sem, next_send, next_recv, mate_send, mate_recv,
+    n_prow, n_pcol, width, coupling, own_shift, panel, inverse, right,
+    across, pivots, shift, work, below, stage, stage_sem, local_sem, next_send, next_recv, mate_send, mate_recv,
     pivot_send, pivot_recv, pivot_local, cross_send, cross_recv, shift_send, shift_recv,
 ):
     p = lax.axis_index("prow")
@@ -211,16 +217,18 @@
             (x <= s) & (x >= 1),
         )
 
+    def cross_start(s, piece):
+        for way, goes in enumerate(ways(s)):
+            @pl.when(goes)
+            def _():
+                cross_copy(s, piece, way).start()
+
     def cross(piece):
         for s in (0, 1):
             @pl.when(p != s)
             def _():
                 cross_copy(s, piece, 0).wait_recv()
-
-            for way, goes in enumerate(ways(s)):
-                @pl.when(goes)
-                def _():
-                    cross_copy(s, piece, way).start()
+                cross_start(s, piece)
 
     forward(0)
     for i in (0, 1):
@@ -238,8 +246,24 @@
                 pivot_copy(i, d, source).start()
             pltpu.make_async_copy(panel.at[source, 0], pivots.at[i], pivot_local.at[i]).start()
 
-    forward(1)
-    forward(2)
+    early = min(3, chunks)
+
+    @pl.loop(1, early)
+    def _(k):
+        forward(k)
+
+    @pl.when(q < 2)
+    def _():
+        @pl.loop(early, chunks)
+        def _(k):
+            forward(k)
+
+    for s in (0, 1):
+        @pl.when(p == s)
+        def _():
+            @pl.loop(0, PIECES)
+            def _(piece):
+                cross_start(s, piece)
 
     def arrived(i, owner, source):
         @pl.when(p == owner)
@@ -259,26 +283,27 @@
         def _():
             shift_copy(i, 1).wait_recv()
 
+    slots = block // (SLOT * GROUP)
+
     def pass_on(slot):
-        k = slot + 3
-
-        @pl.when(k < chunks)
+        k = slot + early
+
+        @pl.when((q >= 2) & (k < chunks))
         def _():
             forward(k)
-            sent(k - 3)
-
-        @pl.when(slot < PIECES)
-        def _():
-            cross(slot)
-
-    slots = block // (2 * GROUP)
+
+        @pl.when((slot >= 2 * slots - PIECES) & (slot < 2 * slots))
+        def _():
+            cross(slot - (2 * slots - PIECES))
 
     def factor(i):
         @pl.loop(0, slots)
         def _(slot):
             pass_on(i * slots + slot)
-            eliminate_group(work, 2 * slot)
-            eliminate_group(work, 2 * slot + 1)
+
+            @pl.loop(0, SLOT)
+            def _(part):
+                eliminate_group(work, slot * SLOT + part)
 
         rows = slice(i * block, (i + 1) * block)
         inverse[rows, rows] = lower_part(work[...])
@@ -301,7 +326,17 @@
         second, dot(below[...], inverse[0:block, 0:block], ((1,), (0,))), ((1,), (0,))
     )
 
-    @pl.loop(2 * slots, max(chunks - 3, 2 * slots))
+    pass_on(2 * slots)
+    panels = [
+        jnp.concatenate([across[s, :, c, :] for c in range(across.shape[2])], axis=1)
+        for s in (0, 1)
+    ]
+    solved = dot(inverse[...], jnp.concatenate(panels, axis=0), ((1,), (0,)))
+    high, low = halves(solved)
+    for j, piece in enumerate((high, low, high)):
+        right[2 * j * block:2 * (j + 1) * block, :] = piece
+
+    @pl.loop(2 * slots + 1, max(chunks - early, 2 * slots + 1))
     def _(slot):
         pass_on(slot)
 
@@ -325,7 +360,7 @@
                 def _():
                     cross_copy(s, piece, way).wait_send()
 
-    @pl.loop(chunks - 3, chunks)
+    @pl.loop(0, chunks)
     def _(k):
         sent(k)
 
@@ -334,28 +369,9 @@
         from_mate(k).wait_recv()
 
 
-def halves(x):
-    high = x.astype(jnp.bfloat16)
-    return high, (x - high.astype(jnp.float32)).astype(jnp.bfloat16)
-
-
-def update_kernel(n_prow, n_pcol, matrix, panel, across, inverse, out, right):
+def update_kernel(n_prow, n_pcol, matrix, panel, inverse, right, out):
     step = pl.program_id(0)
     blocks, size, col_blocks, _ = matrix.shape
-
-    @pl.when(step == 0)
-    def _():
-        panels = [
-            jnp.concatenate(
-                [across[s, pl.ds(c, size, stride=col_blocks), :] for c in range(col_blocks)],
-                axis=1,
-            )
-            for s in (0, 1)
-        ]
-        solved = dot(inverse[...], jnp.concatenate(panels, axis=0), ((1,), (0,)))
-        high, low = halves(solved)
-        for j, piece in enumerate((high, low, high)):
-            right[2 * j * size:2 * (j + 1) * size, :] = piece
 
     raw = jnp.concatenate(
         [panel[s].reshape(blocks * size, size) for s in (0, 1)], axis=1
@@ -380,16 +396,17 @@
     dma = pltpu.SemaphoreType.DMA
     vmem = pl.BlockSpec(memory_space=pltpu.VMEM)
     own_shift = jnp.broadcast_to(diagonal[0], (8, size))
-    panel, across, inverse = pl.pallas_call(
+    panel, inverse, right = pl.pallas_call(
         functools.partial(share_kernel, n_prow, n_pcol, width),
         out_shape=(
             jax.ShapeDtypeStruct((2, chunks, size, size), f32),
-            jax.ShapeDtypeStruct((2, size, col_blocks, size), f32),
             jax.ShapeDtypeStruct((2 * size, 2 * size), f32),
+            jax.ShapeDtypeStruct((6 * size, col_blocks * size), jnp.bfloat16),
         ),
         in_specs=[pl.BlockSpec(memory_space=pl.ANY), vmem],
         out_specs=(vmem,) * 3,
         scratch_shapes=[
+            pltpu.VMEM((2, size, col_blocks, size), f32),
             pltpu.VMEM((3, size, size), f32),
             pltpu.VMEM((2, 8, size), f32),
             pltpu.VMEM((size, size), f32),
@@ -412,14 +429,13 @@
         in_specs=[
             pl.BlockSpec((blocks, size, col_blocks, size), lambda i: (i, 0, 0, 0)),
             pl.BlockSpec((2, blocks, size, size), lambda i: (0, i, 0, 0)),
-            pl.BlockSpec((2, size * col_blocks, size), lambda i: (0, 0, 0)),
             pl.BlockSpec((2 * size, 2 * size), lambda i: (0, 0)),
+            pl.BlockSpec((6 * size, col_blocks * size), lambda i: (0, 0)),
         ],
         out_specs=pl.BlockSpec((blocks, size, col_blocks, size), lambda i: (i, 0, 0, 0)),
-        scratch_shapes=[pltpu.VMEM((6 * size, col_blocks * size), jnp.bfloat16)],
         compiler_params=pltpu.CompilerParams(vmem_limit_bytes=60 * 1024 * 1024),
         name="update_trailing",
-    )(coupling, panel, across.reshape(2, size * col_blocks, size), inverse)
+    )(coupling, panel, inverse, right)
 
 
 def solution(mesh):

time: 86.3 us -> 84.4 us (0.978)
  the two profiles are of different devices: /device:TPU:28 before, /device:TPU:29 now
where the time goes in v4:
time: 84.4 us; the launch traced here: 84.2 us
  Pallas kernels  82.9 us (98%)
  local copies, waits for them, and re-layouts  1.28 us (2%)
    pallas_call x1, Pallas kernels, on_device(): pl.pallas_call(functools.partial(share_kernel, n_prow, n_pcol, width), ou...  69.2 us
    pallas_call x1, Pallas kernels, on_device(): pl.pallas_call(functools.partial(update_kernel, n_prow, n_pcol), grid=(ch...  13.8 us

profile of v4, /device:TPU:29, one launch (start us, length us, event | category | flops | bytes accessed | tf_op | source)
XLA Modules:
  0.0 84.2 jit_solution(9314390267911112355)
XLA Ops:
  0.0 0.7 slice_bitcast_fusion
  0.7 0.6 broadcast_in_dim.3.own_shift
  1.3 69.2 %share_panels.1 = (f32[2,16,128,128]{3,2,1,0:T(8,128)}, f32[256,256]{1,0:T(8,128)}, bf16[768,1024]{1,0:T(8,128)(2,1)}) custom-call(f32[16,128,8,128]{3,2,1,0:T(8,128)} %matrix.1, f32[8,128]{1,0:T(8,128)} %broadcast_in_dim.3.own_shift), custom_call_target="tpu_custom_call" | custom-call | tf_op jit(solution)/shard_map/share_panels/pallas_call | solution.py:399
  70.5 13.8 %update_trailing.1 = f32[16,128,8,128]{3,2,1,0:T(8,128)} custom-call(f32[16,128,8,128]{3,2,1,0:T(8,128)} %matrix.1, f32[2,16,128,128]{3,2,1,0:T(8,128)} %get-tuple-element.8.panel, f32[256,256]{1,0:T(8,128)} %get-tuple-element.9.inverse, bf16[768,1024]{1,0:T(8,128)(2,1)} %get-tuple-element.10.right), custom_call_target="tpu_custom_call" | custom-call | tf_op jit(solution)/shard_map/update_trailing/pallas_call | solution.py:425

commit v5 on v4

--- a/solution.py
+++ b/solution.py
@@ -12,7 +12,8 @@
 MESH = pl.DeviceIdType.MESH
 GROUP = 8
 PIECES = 4
-SLOT = 4
+SLOT = 2
+QUICK = 4
 
 
 def dot(a, b, contract):
@@ -84,8 +85,8 @@
 
 
 def share_kernel(
-    n_prow, n_pcol, width, coupling, own_shift, panel, inverse, right,
-    across, pivots, shift, work, below, stage, stage_sem, local_sem, next_send, next_recv, mate_send, mate_recv,
+    n_prow, n_pcol, width, coupling, diagonal, left, right,
+    panel, inverse, across, pivots, shift, work, below, stage, stage_sem, local_sem, next_send, next_recv, mate_send, mate_recv,
     pivot_send, pivot_recv, pivot_local, cross_send, cross_recv, shift_send, shift_recv,
 ):
     p = lax.axis_index("prow")
@@ -192,13 +193,13 @@
 
     def shift_copy(i, d):
         return pltpu.make_async_remote_copy(
-            src_ref=own_shift, dst_ref=shift.at[i],
+            src_ref=diagonal.at[0:8], dst_ref=shift.at[i],
             send_sem=shift_send.at[i, d], recv_sem=shift_recv.at[i],
             device_id={"prow": (p + d) % n_prow}, device_id_type=MESH,
         )
 
     def shift_local(i):
-        return pltpu.make_async_copy(own_shift, shift.at[i], local_sem.at[2 + i])
+        return pltpu.make_async_copy(diagonal.at[0:8], shift.at[i], local_sem.at[2 + i])
 
     def cross_copy(s, piece, way):
         rows = block // PIECES
@@ -223,13 +224,23 @@
             def _():
                 cross_copy(s, piece, way).start()
 
-    def cross(piece):
+    def passes_on(s):
+        first, second, third = ways(s)
+        return first | second | third
+
+    def cross_relay(piece):
         for s in (0, 1):
-            @pl.when(p != s)
+            @pl.when((p != s) & passes_on(s))
             def _():
                 cross_copy(s, piece, 0).wait_recv()
                 cross_start(s, piece)
 
+    def cross_end(piece):
+        for s in (0, 1):
+            @pl.when((p != s) & jnp.logical_not(passes_on(s)))
+            def _():
+                cross_copy(s, piece, 0).wait_recv()
+
     forward(0)
     for i in (0, 1):
         @pl.when(p == i)
@@ -286,15 +297,15 @@
     slots = block // (SLOT * GROUP)
 
     def pass_on(slot):
-        k = slot + early
-
-        @pl.when((q >= 2) & (k < chunks))
+        k = early + jnp.where(slot < QUICK, slot, (slot + QUICK) // 2)
+
+        @pl.when((q >= 2) & (k < chunks) & ((slot < QUICK) | (slot % 2 == 0)))
         def _():
             forward(k)
 
-        @pl.when((slot >= 2 * slots - PIECES) & (slot < 2 * slots))
-        def _():
-            cross(slot - (2 * slots - PIECES))
+        @pl.when((slot % 3 == 0) & (slot >= 3) & (slot < 3 + 3 * PIECES))
+        def _():
+            cross_relay(slot // 3 - 1)
 
     def factor(i):
         @pl.loop(0, slots)
@@ -326,7 +337,10 @@
         second, dot(below[...], inverse[0:block, 0:block], ((1,), (0,))), ((1,), (0,))
     )
 
-    pass_on(2 * slots)
+    @pl.loop(0, PIECES)
+    def _(piece):
+        cross_end(piece)
+
     panels = [
         jnp.concatenate([across[s, :, c, :] for c in range(across.shape[2])], axis=1)
         for s in (0, 1)
@@ -336,9 +350,29 @@
     for j, piece in enumerate((high, low, high)):
         right[2 * j * block:2 * (j + 1) * block, :] = piece
 
-    @pl.loop(2 * slots + 1, max(chunks - early, 2 * slots + 1))
-    def _(slot):
-        pass_on(slot)
+    done = min(early + (2 * slots + QUICK) // 2, chunks)
+
+    @pl.loop(0, chunks // 2)
+    def _(pair):
+        for k in (2 * pair, 2 * pair + 1):
+            @pl.when((q >= 2) & (k + done < chunks))
+            def _():
+                forward(k + done)
+
+            @pl.when(k > 0)
+            def _():
+                from_mate(k).wait_recv()
+
+        raw = jnp.concatenate(
+            [
+                jnp.concatenate([panel[0, k], panel[1, k]], axis=1)
+                for k in (2 * pair, 2 * pair + 1)
+            ],
+            axis=0,
+        )
+        solved_rows = jnp.concatenate(halves(dot(raw, inverse[...], ((1,), (1,)))), axis=1)
+        left[2 * pair] = solved_rows[0:block]
+        left[2 * pair + 1] = solved_rows[block:]
 
     for i, owner, source in parts:
         @pl.when(p == owner)
@@ -364,21 +398,14 @@
     def _(k):
         sent(k)
 
-    @pl.loop(1, chunks)
-    def _(k):
-        from_mate(k).wait_recv()
-
-
-def update_kernel(n_prow, n_pcol, matrix, panel, inverse, right, out):
+
+def update_kernel(n_prow, n_pcol, matrix, left, right, out):
     step = pl.program_id(0)
     blocks, size, col_blocks, _ = matrix.shape
 
-    raw = jnp.concatenate(
-        [panel[s].reshape(blocks * size, size) for s in (0, 1)], axis=1
-    )
-    high, low = halves(dot(raw, inverse[...], ((1,), (1,))))
-    left = jnp.concatenate([high, high, low], axis=1)
-    product = jnp.dot(left, right[...], preferred_element_type=jnp.float32)
+    rows = left[...].reshape(blocks * size, 4 * size)
+    rows = jnp.concatenate([rows[:, 0:2 * size], rows], axis=1)
+    product = jnp.dot(rows, right[...], preferred_element_type=jnp.float32)
     product = product.reshape(blocks, size, col_blocks, size)
     p = lax.axis_index("prow")
     col = lax.broadcasted_iota(jnp.int32, (1, col_blocks, size), 1) * n_pcol
@@ -395,17 +422,17 @@
     f32 = jnp.float32
     dma = pltpu.SemaphoreType.DMA
     vmem = pl.BlockSpec(memory_space=pltpu.VMEM)
-    own_shift = jnp.broadcast_to(diagonal[0], (8, size))
-    panel, inverse, right = pl.pallas_call(
+    left, right = pl.pallas_call(
         functools.partial(share_kernel, n_prow, n_pcol, width),
         out_shape=(
-            jax.ShapeDtypeStruct((2, chunks, size, size), f32),
-            jax.ShapeDtypeStruct((2 * size, 2 * size), f32),
+            jax.ShapeDtypeStruct((chunks, size, 4 * size), jnp.bfloat16),
             jax.ShapeDtypeStruct((6 * size, col_blocks * size), jnp.bfloat16),
         ),
         in_specs=[pl.BlockSpec(memory_space=pl.ANY), vmem],
-        out_specs=(vmem,) * 3,
+        out_specs=(vmem,) * 2,
         scratch_shapes=[
+            pltpu.VMEM((2, chunks, size, size), f32),
+            pltpu.VMEM((2 * size, 2 * size), f32),
             pltpu.VMEM((2, size, col_blocks, size), f32),
             pltpu.VMEM((3, size, size), f32),
             pltpu.VMEM((2, 8, size), f32),
@@ -420,7 +447,7 @@
             collective_id=0, has_side_effects=True, vmem_limit_bytes=60 * 1024 * 1024
         ),
         name="share_panels",
-    )(coupling, own_shift)
+    )(coupling, diagonal)
     blocks = math.gcd(chunks, 4)
     return pl.pallas_call(
         functools.partial(update_kernel, n_prow, n_pcol),
@@ -428,14 +455,13 @@
         out_shape=jax.ShapeDtypeStruct(coupling.shape, f32),
         in_specs=[
             pl.BlockSpec((blocks, size, col_blocks, size), lambda i: (i, 0, 0, 0)),
-            pl.BlockSpec((2, blocks, size, size), lambda i: (0, i, 0, 0)),
-            pl.BlockSpec((2 * size, 2 * size), lambda i: (0, 0)),
+            pl.BlockSpec((blocks, size, 4 * size), lambda i: (i, 0, 0)),
             pl.BlockSpec((6 * size, col_blocks * size), lambda i: (0, 0)),
         ],
         out_specs=pl.BlockSpec((blocks, size, col_blocks, size), lambda i: (i, 0, 0, 0)),
         compiler_params=pltpu.CompilerParams(vmem_limit_bytes=60 * 1024 * 1024),
         name="update_trailing",
-    )(coupling, panel, inverse, right)
+    )(coupling, left, right)
 
 
 def solution(mesh):

time: 84.4 us -> 57.2 us (0.68)
  Pallas kernels: 82.9 us -> 56.4 us
  local copies, waits for them, and re-layouts: 1.28 us -> 0 us
    pallas_call x1, Pallas kernels: 69.2 us -> 45.9 us  [on_device(): pl.pallas_call(functools.partial(share_kernel, n_prow, n_pcol, width), ou...]
    pallas_call x1, Pallas kernels: 13.8 us -> 10.4 us  [on_device(): pl.pallas_call(functools.partial(update_kernel, n_prow, n_pcol), grid=(ch...]
where the time goes in v5:
time: 57.2 us; the launch traced here: 56.4 us
  Pallas kernels  56.4 us (99%)
    pallas_call x1, Pallas kernels, on_device(): pl.pallas_call(functools.partial(share_kernel, n_prow, n_pcol, width), ou...  45.9 us
    pallas_call x1, Pallas kernels, on_device(): pl.pallas_call(functools.partial(update_kernel, n_prow, n_pcol), grid=(ch...  10.4 us

profile of v5, /device:TPU:29, one launch (start us, length us, event | category | flops | bytes accessed | tf_op | source)
XLA Modules:
  0.0 56.4 jit_solution(4812819765246872013)
XLA Ops:
  0.0 45.9 %share_panels.1 = (bf16[16,128,512]{2,1,0:T(8,128)(2,1)}, bf16[768,1024]{1,0:T(8,128)(2,1)}) custom-call(f32[16,128,8,128]{3,2,1,0:T(8,128)} %matrix.1, f32[16,128]{1,0:T(8,128)} %diagonal.1), custom_call_target="tpu_custom_call" | custom-call | tf_op jit(solution)/shard_map/share_panels/pallas_call | solution.py:425
  45.9 10.4 %update_trailing.1 = f32[16,128,8,128]{3,2,1,0:T(8,128)} custom-call(f32[16,128,8,128]{3,2,1,0:T(8,128)} %matrix.1, bf16[16,128,512]{2,1,0:T(8,128)(2,1)} %get-tuple-element.7.left, bf16[768,1024]{1,0:T(8,128)(2,1)} %get-tuple-element.8.right), custom_call_target="tpu_custom_call" | custom-call | tf_op jit(solution)/shard_map/update_trailing/pallas_call | solution.py:452

commit v6 on v5

--- a/solution.py
+++ b/solution.py
@@ -13,7 +13,8 @@
 GROUP = 8
 PIECES = 4
 SLOT = 2
-QUICK = 4
+QUICK = 6
+AHEAD = 4
 
 
 def dot(a, b, contract):
@@ -86,7 +87,8 @@
 
 def share_kernel(
     n_prow, n_pcol, width, coupling, diagonal, left, right,
-    panel, inverse, across, pivots, shift, work, below, stage, stage_sem, local_sem, next_send, next_recv, mate_send, mate_recv,
+    left_own, right_own, panel, inverse, across, pivots, shift, work, below, stage,
+    left_sem, stage_sem, local_sem, next_send, next_recv, mate_send, mate_recv,
     pivot_send, pivot_recv, pivot_local, cross_send, cross_recv, shift_send, shift_recv,
 ):
     p = lax.axis_index("prow")
@@ -257,11 +259,9 @@
                 pivot_copy(i, d, source).start()
             pltpu.make_async_copy(panel.at[source, 0], pivots.at[i], pivot_local.at[i]).start()
 
-    early = min(3, chunks)
-
-    @pl.loop(1, early)
-    def _(k):
-        forward(k)
+    early = 1
+    middle = (q >= 2) & (q + 2 < n_pcol)
+    last = (q >= 2) & (q + 2 >= n_pcol)
 
     @pl.when(q < 2)
     def _():
@@ -299,7 +299,7 @@
     def pass_on(slot):
         k = early + jnp.where(slot < QUICK, slot, (slot + QUICK) // 2)
 
-        @pl.when((q >= 2) & (k < chunks) & ((slot < QUICK) | (slot % 2 == 0)))
+        @pl.when(middle & (k < chunks) & ((slot < QUICK) | (slot % 2 == 0)))
         def _():
             forward(k)
 
@@ -333,9 +333,19 @@
         below[...], below[...], ((1,), (1,))
     )
     second = factor(1)
+    done = min(early + (2 * slots + QUICK) // 2, chunks)
+
+    def forward_middle(start, stop):
+        for k in range(min(start, chunks), min(stop, chunks)):
+            @pl.when(middle)
+            def _():
+                forward(k)
+
+    forward_middle(done, done + 2)
     inverse[block:, 0:block] = -dot(
         second, dot(below[...], inverse[0:block, 0:block], ((1,), (0,))), ((1,), (0,))
     )
+    forward_middle(done + 2, done + 3)
 
     @pl.loop(0, PIECES)
     def _(piece):
@@ -348,16 +358,27 @@
     solved = dot(inverse[...], jnp.concatenate(panels, axis=0), ((1,), (0,)))
     high, low = halves(solved)
     for j, piece in enumerate((high, low, high)):
-        right[2 * j * block:2 * (j + 1) * block, :] = piece
-
-    done = min(early + (2 * slots + QUICK) // 2, chunks)
+        right_own[2 * j * block:2 * (j + 1) * block, :] = piece
+    right_copy = pltpu.make_async_copy(right_own, right, local_sem.at[0])
+    right_copy.start()
+    forward_middle(done + 3, chunks)
+
+    @pl.when(last)
+    def _():
+        @pl.loop(early, done)
+        def _(k):
+            forward(k)
+
+    def left_copy(pair):
+        part = pl.ds(2 * pair, 2)
+        return pltpu.make_async_copy(left_own.at[part], left.at[part], left_sem.at[pair])
 
     @pl.loop(0, chunks // 2)
     def _(pair):
         for k in (2 * pair, 2 * pair + 1):
-            @pl.when((q >= 2) & (k + done < chunks))
+            @pl.when(last & (k + AHEAD >= done) & (k + AHEAD < chunks))
             def _():
-                forward(k + done)
+                forward(k + AHEAD)
 
             @pl.when(k > 0)
             def _():
@@ -371,8 +392,9 @@
             axis=0,
         )
         solved_rows = jnp.concatenate(halves(dot(raw, inverse[...], ((1,), (1,)))), axis=1)
-        left[2 * pair] = solved_rows[0:block]
-        left[2 * pair + 1] = solved_rows[block:]
+        left_own[2 * pair] = solved_rows[0:block]
+        left_own[2 * pair + 1] = solved_rows[block:]
+        left_copy(pair).start()
 
     for i, owner, source in parts:
         @pl.when(p == owner)
@@ -397,6 +419,12 @@
     @pl.loop(0, chunks)
     def _(k):
         sent(k)
+
+    right_copy.wait()
+
+    @pl.loop(0, chunks // 2)
+    def _(pair):
+        left_copy(pair).wait()
 
 
 def update_kernel(n_prow, n_pcol, matrix, left, right, out):
@@ -429,8 +457,10 @@
             jax.ShapeDtypeStruct((6 * size, col_blocks * size), jnp.bfloat16),
         ),
         in_specs=[pl.BlockSpec(memory_space=pl.ANY), vmem],
-        out_specs=(vmem,) * 2,
+        out_specs=(pl.BlockSpec(memory_space=pl.ANY),) * 2,
         scratch_shapes=[
+            pltpu.VMEM((chunks, size, 4 * size), jnp.bfloat16),
+            pltpu.VMEM((6 * size, col_blocks * size), jnp.bfloat16),
             pltpu.VMEM((2, chunks, size, size), f32),
             pltpu.VMEM((2 * size, 2 * size), f32),
             pltpu.VMEM((2, size, col_blocks, size), f32),
@@ -439,7 +469,7 @@
             pltpu.VMEM((size, size), f32),
             pltpu.VMEM((size, size), f32),
             pltpu.VMEM(coupling.shape, f32),
-            dma((chunks,)), dma((4,)), dma((chunks,)), dma((chunks,)), dma((chunks,)), dma((chunks,)),
+            dma((chunks // 2,)), dma((chunks,)), dma((4,)), dma((chunks,)), dma((chunks,)), dma((chunks,)), dma((chunks,)),
             dma((3, n_prow)), dma((3,)), dma((3,)),
             dma((2, PIECES, 3)), dma((2, PIECES)), dma((2, n_prow)), dma((2,)),
         ],
@@ -448,7 +478,7 @@
         ),
         name="share_panels",
     )(coupling, diagonal)
-    blocks = math.gcd(chunks, 4)
+    blocks = math.gcd(chunks, 2)
     return pl.pallas_call(
         functools.partial(update_kernel, n_prow, n_pcol),
         grid=(chunks // blocks,),

time: 57.2 us -> 56.2 us (0.983)
  Pallas kernels: 56.4 us -> 55.8 us
    pallas_call x1, Pallas kernels: 45.9 us -> 44.2 us  [on_device(): pl.pallas_call(functools.partial(share_kernel, n_prow, n_pcol, width), ou...]
    pallas_call x1, Pallas kernels: 10.4 us -> 11.6 us  [on_device(): pl.pallas_call(functools.partial(update_kernel, n_prow, n_pcol), grid=(ch...]
where the time goes in v6:
time: 56.2 us; the launch traced here: 55.8 us
  Pallas kernels  55.8 us (99%)
    pallas_call x1, Pallas kernels, on_device(): pl.pallas_call(functools.partial(share_kernel, n_prow, n_pcol, width), ou...  44.2 us
    pallas_call x1, Pallas kernels, on_device(): pl.pallas_call(functools.partial(update_kernel, n_prow, n_pcol), grid=(ch...  11.6 us

profile of v6, /device:TPU:29, one launch (start us, length us, event | category | flops | bytes accessed | tf_op | source)
XLA Modules:
  0.0 55.8 jit_solution(461476012428534312)
XLA Ops:
  0.0 44.2 %share_panels.1 = (bf16[16,128,512]{2,1,0:T(8,128)(2,1)}, bf16[768,1024]{1,0:T(8,128)(2,1)}) custom-call(f32[16,128,8,128]{3,2,1,0:T(8,128)} %matrix.1, f32[16,128]{1,0:T(8,128)} %diagonal.1), custom_call_target="tpu_custom_call" | custom-call | tf_op jit(solution)/shard_map/share_panels/pallas_call | solution.py:453
  44.2 11.6 %update_trailing.1 = f32[16,128,8,128]{3,2,1,0:T(8,128)} custom-call(f32[16,128,8,128]{3,2,1,0:T(8,128)} %matrix.1, bf16[16,128,512]{2,1,0:T(8,128)(2,1)} %get-tuple-element.7.left, bf16[768,1024]{1,0:T(8,128)(2,1)} %get-tuple-element.8.right), custom_call_target="tpu_custom_call" | custom-call | tf_op jit(solution)/shard_map/update_trailing/pallas_call | solution.py:482

commit v7 on v6

--- a/solution.py
+++ b/solution.py
@@ -14,7 +14,7 @@
 PIECES = 4
 SLOT = 2
 QUICK = 6
-AHEAD = 4
+CROSS = 2
 
 
 def dot(a, b, contract):
@@ -269,13 +269,6 @@
         def _(k):
             forward(k)
 
-    for s in (0, 1):
-        @pl.when(p == s)
-        def _():
-            @pl.loop(0, PIECES)
-            def _(piece):
-                cross_start(s, piece)
-
     def arrived(i, owner, source):
         @pl.when(p == owner)
         def _():
@@ -303,9 +296,16 @@
         def _():
             forward(k)
 
-        @pl.when((slot % 3 == 0) & (slot >= 3) & (slot < 3 + 3 * PIECES))
-        def _():
-            cross_relay(slot // 3 - 1)
+        for s in (0, 1):
+            @pl.when((p == s) & (slot == CROSS))
+            def _():
+                @pl.loop(0, PIECES)
+                def _(piece):
+                    cross_start(s, piece)
+
+        @pl.when((slot % 4 == 3) & (slot >= CROSS + 4))
+        def _():
+            cross_relay((slot - CROSS) // 4 - 1)
 
     def factor(i):
         @pl.loop(0, slots)
@@ -341,11 +341,55 @@
             def _():
                 forward(k)
 
-    forward_middle(done, done + 2)
+    relayed = (2 * slots - CROSS - 1) // 4
+    forward_middle(done, done + 1)
     inverse[block:, 0:block] = -dot(
         second, dot(below[...], inverse[0:block, 0:block], ((1,), (0,))), ((1,), (0,))
     )
-    forward_middle(done + 2, done + 3)
+
+    @pl.loop(relayed, PIECES)
+    def _(piece):
+        cross_relay(piece)
+
+    @pl.when(last)
+    def _():
+        @pl.loop(early, done)
+        def _(k):
+            forward(k)
+
+    def left_copy(pair):
+        part = pl.ds(2 * pair, 2)
+        return pltpu.make_async_copy(left_own.at[part], left.at[part], left_sem.at[pair])
+
+    def solve_rows(pair):
+        @pl.when(middle & (pair + done + 1 < chunks))
+        def _():
+            forward(pair + done + 1)
+
+        for k in (2 * pair, 2 * pair + 1):
+            @pl.when(last & (k >= done))
+            def _():
+                forward(k)
+
+            @pl.when(k > 0)
+            def _():
+                from_mate(k).wait_recv()
+
+        raw = jnp.concatenate(
+            [
+                jnp.concatenate([panel[0, k], panel[1, k]], axis=1)
+                for k in (2 * pair, 2 * pair + 1)
+            ],
+            axis=0,
+        )
+        solved_rows = jnp.concatenate(halves(dot(raw, inverse[...], ((1,), (1,)))), axis=1)
+        left_own[2 * pair] = solved_rows[0:block]
+        left_own[2 * pair + 1] = solved_rows[block:]
+        left_copy(pair).start()
+
+    @pl.loop(0, done // 2)
+    def _(pair):
+        solve_rows(pair)
 
     @pl.loop(0, PIECES)
     def _(piece):
@@ -361,40 +405,10 @@
         right_own[2 * j * block:2 * (j + 1) * block, :] = piece
     right_copy = pltpu.make_async_copy(right_own, right, local_sem.at[0])
     right_copy.start()
-    forward_middle(done + 3, chunks)
-
-    @pl.when(last)
-    def _():
-        @pl.loop(early, done)
-        def _(k):
-            forward(k)
-
-    def left_copy(pair):
-        part = pl.ds(2 * pair, 2)
-        return pltpu.make_async_copy(left_own.at[part], left.at[part], left_sem.at[pair])
-
-    @pl.loop(0, chunks // 2)
+
+    @pl.loop(done // 2, chunks // 2)
     def _(pair):
-        for k in (2 * pair, 2 * pair + 1):
-            @pl.when(last & (k + AHEAD >= done) & (k + AHEAD < chunks))
-            def _():
-                forward(k + AHEAD)
-
-            @pl.when(k > 0)
-            def _():
-                from_mate(k).wait_recv()
-
-        raw = jnp.concatenate(
-            [
-                jnp.concatenate([panel[0, k], panel[1, k]], axis=1)
-                for k in (2 * pair, 2 * pair + 1)
-            ],
-            axis=0,
-        )
-        solved_rows = jnp.concatenate(halves(dot(raw, inverse[...], ((1,), (1,)))), axis=1)
-        left_own[2 * pair] = solved_rows[0:block]
-        left_own[2 * pair + 1] = solved_rows[block:]
-        left_copy(pair).start()
+        solve_rows(pair)
 
     for i, owner, source in parts:
         @pl.when(p == owner)
@@ -478,7 +492,7 @@
         ),
         name="share_panels",
     )(coupling, diagonal)
-    blocks = math.gcd(chunks, 2)
+    blocks = math.gcd(chunks, 4)
     return pl.pallas_call(
         functools.partial(update_kernel, n_prow, n_pcol),
         grid=(chunks // blocks,),

time: 56.2 us -> 56.1 us (level)
    pallas_call x1, Pallas kernels: 44.2 us -> 45.5 us  [on_device(): pl.pallas_call(functools.partial(share_kernel, n_prow, n_pcol, width), ou...]
    pallas_call x1, Pallas kernels: 11.6 us -> 10.4 us  [on_device(): pl.pallas_call(functools.partial(update_kernel, n_prow, n_pcol), grid=(ch...]
where the time goes in v7:
time: 56.1 us; the launch traced here: 55.9 us
  Pallas kernels  55.9 us (100%)
    pallas_call x1, Pallas kernels, on_device(): pl.pallas_call(functools.partial(share_kernel, n_prow, n_pcol, width), ou...  45.5 us
    pallas_call x1, Pallas kernels, on_device(): pl.pallas_call(functools.partial(update_kernel, n_prow, n_pcol), grid=(ch...  10.4 us

profile of v7, /device:TPU:29, one launch (start us, length us, event | category | flops | bytes accessed | tf_op | source)
XLA Modules:
  0.0 55.9 jit_solution(12305806044956868254)
XLA Ops:
  0.0 45.5 %share_panels.1 = (bf16[16,128,512]{2,1,0:T(8,128)(2,1)}, bf16[768,1024]{1,0:T(8,128)(2,1)}) custom-call(f32[16,128,8,128]{3,2,1,0:T(8,128)} %matrix.1, f32[16,128]{1,0:T(8,128)} %diagonal.1), custom_call_target="tpu_custom_call" | custom-call | tf_op jit(solution)/shard_map/share_panels/pallas_call | solution.py:467
  45.5 10.4 %update_trailing.1 = f32[16,128,8,128]{3,2,1,0:T(8,128)} custom-call(f32[16,128,8,128]{3,2,1,0:T(8,128)} %matrix.1, bf16[16,128,512]{2,1,0:T(8,128)(2,1)} %get-tuple-element.7.left, bf16[768,1024]{1,0:T(8,128)(2,1)} %get-tuple-element.8.right), custom_call_target="tpu_custom_call" | custom-call | tf_op jit(solution)/shard_map/update_trailing/pallas_call | solution.py:496

commit v8 on v7

--- a/solution.py
+++ b/solution.py
@@ -90,6 +90,7 @@
     left_own, right_own, panel, inverse, across, pivots, shift, work, below, stage,
     left_sem, stage_sem, local_sem, next_send, next_recv, mate_send, mate_recv,
     pivot_send, pivot_recv, pivot_local, cross_send, cross_recv, shift_send, shift_recv,
+    first_send,
 ):
     p = lax.axis_index("prow")
     q = lax.axis_index("pcol")
@@ -119,6 +120,18 @@
     def staged(k):
         return pltpu.make_async_copy(coupling.at[k], stage.at[k], stage_sem.at[k])
 
+    chips = n_pcol // 2
+    for d in range(2, chips):
+        @pl.when(q < 2)
+        def _():
+            pl.semaphore_signal(
+                barrier, inc=1, device_id={"pcol": side + 2 * d}, device_id_type=MESH
+            )
+
+    @pl.when(q >= 4)
+    def _():
+        pl.semaphore_signal(barrier, inc=1, device_id={"pcol": side}, device_id_type=MESH)
+
     own_across = pltpu.make_async_copy(coupling.at[0], across.at[p % 2], local_sem.at[1])
 
     @pl.when(q < 2)
@@ -137,7 +150,8 @@
 
     pl.semaphore_wait(
         barrier,
-        n_prow + jnp.where(q >= 2, 1, 0) + jnp.where(q + 2 < n_pcol, 1, 0),
+        n_prow + jnp.where(q >= 2, 1, 0) + jnp.where(q + 2 < n_pcol, 1, 0)
+        + jnp.where(q < 2, max(chips - 2, 0), 0) + jnp.where(q >= 4, 1, 0),
     )
 
     def to_next(k):
@@ -176,6 +190,46 @@
             to_next(k).start()
 
         to_mate(k).start()
+
+    def first_to(d):
+        return pltpu.make_async_remote_copy(
+            src_ref=panel.at[side, 0], dst_ref=panel.at[side, 0],
+            send_sem=first_send.at[d], recv_sem=next_recv.at[0],
+            device_id={"pcol": side + 2 * d}, device_id_type=MESH,
+        )
+
+    def forward_first():
+        @pl.when(q < 2)
+        def _():
+            staged(0).wait()
+            panel[side, 0] = stage[0, :, 0, :]
+
+        @pl.when(q >= 2)
+        def _():
+            to_next(0).wait_recv()
+
+        @pl.when((q < 2) & (p < 2))
+        def _():
+            for d in range(chips - 1, 0, -1):
+                first_to(d).start()
+
+        @pl.when((p >= 2) & (q + 2 < n_pcol))
+        def _():
+            to_next(0).start()
+
+        to_mate(0).start()
+
+    def sent_first():
+        @pl.when((q < 2) & (p < 2))
+        def _():
+            for d in range(1, chips):
+                first_to(d).wait_send()
+
+        @pl.when((p >= 2) & (q + 2 < n_pcol))
+        def _():
+            to_next(0).wait_send()
+
+        to_mate(0).wait_send()
 
     def sent(k):
         @pl.when(q + 2 < n_pcol)
@@ -243,7 +297,7 @@
             def _():
                 cross_copy(s, piece, 0).wait_recv()
 
-    forward(0)
+    forward_first()
     for i in (0, 1):
         @pl.when(p == i)
         def _():
@@ -430,7 +484,9 @@
                 def _():
                     cross_copy(s, piece, way).wait_send()
 
-    @pl.loop(0, chunks)
+    sent_first()
+
+    @pl.loop(1, chunks)
     def _(k):
         sent(k)
 
@@ -485,7 +541,7 @@
             pltpu.VMEM(coupling.shape, f32),
             dma((chunks // 2,)), dma((chunks,)), dma((4,)), dma((chunks,)), dma((chunks,)), dma((chunks,)), dma((chunks,)),
             dma((3, n_prow)), dma((3,)), dma((3,)),
-            dma((2, PIECES, 3)), dma((2, PIECES)), dma((2, n_prow)), dma((2,)),
+            dma((2, PIECES, 3)), dma((2, PIECES)), dma((2, n_prow)), dma((2,)), dma((n_pcol // 2,)),
         ],
         compiler_params=pltpu.CompilerParams(
             collective_id=0, has_side_effects=True, vmem_limit_bytes=60 * 1024 * 1024

time: 56.1 us -> 58.8 us (1.048)
  Pallas kernels: 55.9 us -> 58.3 us
    pallas_call x1, Pallas kernels: 45.5 us -> 47.8 us  [on_device(): pl.pallas_call(functools.partial(share_kernel, n_prow, n_pcol, width), ou...]
where the time goes in v8:
time: 58.8 us; the launch traced here: 58.3 us
  Pallas kernels  58.3 us (99%)
    pallas_call x1, Pallas kernels, on_device(): pl.pallas_call(functools.partial(share_kernel, n_prow, n_pcol, width), ou...  47.8 us
    pallas_call x1, Pallas kernels, on_device(): pl.pallas_call(functools.partial(update_kernel, n_prow, n_pcol), grid=(ch...  10.4 us

profile of v8, /device:TPU:29, one launch (start us, length us, event | category | flops | bytes accessed | tf_op | source)
XLA Modules:
  0.0 58.3 jit_solution(11641258353362922710)
XLA Ops:
  0.0 47.8 %share_panels.1 = (bf16[16,128,512]{2,1,0:T(8,128)(2,1)}, bf16[768,1024]{1,0:T(8,128)(2,1)}) custom-call(f32[16,128,8,128]{3,2,1,0:T(8,128)} %matrix.1, f32[16,128]{1,0:T(8,128)} %diagonal.1), custom_call_target="tpu_custom_call" | custom-call | tf_op jit(solution)/shard_map/share_panels/pallas_call | solution.py:523
  47.8 10.4 %update_trailing.1 = f32[16,128,8,128]{3,2,1,0:T(8,128)} custom-call(f32[16,128,8,128]{3,2,1,0:T(8,128)} %matrix.1, bf16[16,128,512]{2,1,0:T(8,128)(2,1)} %get-tuple-element.7.left, bf16[768,1024]{1,0:T(8,128)(2,1)} %get-tuple-element.8.right), custom_call_target="tpu_custom_call" | custom-call | tf_op jit(solution)/shard_map/update_trailing/pallas_call | solution.py:552

commit v9 on v7

--- a/solution.py
+++ b/solution.py
@@ -244,6 +244,14 @@
                 cross_copy(s, piece, 0).wait_recv()
 
     forward(0)
+    chunks_first = min(4, chunks)
+
+    @pl.when(q < 2)
+    def _():
+        @pl.loop(1, chunks_first)
+        def _(k):
+            forward(k)
+
     for i in (0, 1):
         @pl.when(p == i)
         def _():
@@ -265,7 +273,7 @@
 
     @pl.when(q < 2)
     def _():
-        @pl.loop(early, chunks)
+        @pl.loop(chunks_first, chunks)
         def _(k):
             forward(k)
 

time: 56.1 us -> 56.5 us (level)
  no operation moved by 1% of the time
where the time goes in v9:
time: 56.5 us; the launch traced here: 56.3 us
  Pallas kernels  56.3 us (100%)
    pallas_call x1, Pallas kernels, on_device(): pl.pallas_call(functools.partial(share_kernel, n_prow, n_pcol, width), ou...  45.8 us
    pallas_call x1, Pallas kernels, on_device(): pl.pallas_call(functools.partial(update_kernel, n_prow, n_pcol), grid=(ch...  10.4 us

profile of v9, /device:TPU:29, one launch (start us, length us, event | category | flops | bytes accessed | tf_op | source)
XLA Modules:
  0.0 56.3 jit_solution(6226077144172323852)
XLA Ops:
  0.0 45.8 %share_panels.1 = (bf16[16,128,512]{2,1,0:T(8,128)(2,1)}, bf16[768,1024]{1,0:T(8,128)(2,1)}) custom-call(f32[16,128,8,128]{3,2,1,0:T(8,128)} %matrix.1, f32[16,128]{1,0:T(8,128)} %diagonal.1), custom_call_target="tpu_custom_call" | custom-call | tf_op jit(solution)/shard_map/share_panels/pallas_call | solution.py:475
  45.9 10.4 %update_trailing.1 = f32[16,128,8,128]{3,2,1,0:T(8,128)} custom-call(f32[16,128,8,128]{3,2,1,0:T(8,128)} %matrix.1, bf16[16,128,512]{2,1,0:T(8,128)(2,1)} %get-tuple-element.7.left, bf16[768,1024]{1,0:T(8,128)(2,1)} %get-tuple-element.8.right), custom_call_target="tpu_custom_call" | custom-call | tf_op jit(solution)/shard_map/update_trailing/pallas_call | solution.py:504
